TPU v7x, 128 devices: a whole 4x4x4 slice. The times are simulated.
128 devices in a mesh: seq: 4 (over z), shard: 8 (over x, core), grp: 4 (over y).
Axes of the slice: x: 4, y: 4, z: 4, core: 2. Of those that a mesh axis runs over, the one named last changes fastest.
Arguments:
- tokens: bfloat16 [4, 8, 512, 2048], P('grp', 'shard', 'seq'), may hold values from -6 to 6
- seq_lengths: int32 [4, 6], P('grp'), may hold values from 1 to 2048, 4096 in all within a row
- seq_order: int32 [4, 6], P('grp'), may hold values from 0 to 5, each once within a row
- norm_gain: bfloat16 [2048], P(('seq', 'shard')), may hold values from 0.5 to 1.5
- query_weight: bfloat16 [2048, 2048], P(('seq', 'shard')), may hold values from -0.125 to 0.125
- key_value_weight: bfloat16 [2048, 256], P(('seq', 'shard')), may hold values from -0.125 to 0.125
- out_weight: bfloat16 [2048, 2048], P(('seq', 'shard')), may hold values from -1 to 1
- mlp_gain: bfloat16 [2048], P(('seq', 'shard')), may hold values from 0.5 to 1.5
- gate_weight: bfloat16 [2048, 6144], P(('seq', 'shard')), may hold values from -0.125 to 0.125
- up_weight: bfloat16 [2048, 6144], P(('seq', 'shard')), may hold values from -0.125 to 0.125
- down_weight: bfloat16 [6144, 2048], P(('seq', 'shard')), may hold values from -0.078125 to 0.078125
- cotangent: bfloat16 [4, 8, 512, 2048], P('grp', 'shard', 'seq'), may hold values from -6 to 6
Outputs:
- layer_output: bfloat16 [4, 8, 512, 2048], P('grp', 'shard', 'seq')
- input_grad: float32 [4, 8, 512, 2048], P('grp', 'shard', 'seq')
- norm_gain_grad: float32 [2048], P(('seq', 'shard'))
- query_weight_grad: float32 [2048, 2048], P(('seq', 'shard'))
- key_value_weight_grad: float32 [2048, 256], P(('seq', 'shard'))
- out_weight_grad: float32 [2048, 2048], P(('seq', 'shard'))
- mlp_gain_grad: float32 [2048], P(('seq', 'shard'))
- gate_weight_grad: float32 [2048, 6144], P(('seq', 'shard'))
- up_weight_grad: float32 [2048, 6144], P(('seq', 'shard'))
- down_weight_grad: float32 [6144, 2048], P(('seq', 'shard'))
All inputs are finite; a program needn't handle non-finite values.
Results may differ from a plain program's by a relative error of at most 0.028.
Values may be sent and summed in bfloat16 or wider, within the bound.
No kernel may reach another device: no remote copies, remote signals or barrier semaphores. Data moves between devices by JAX's collectives and lax.ppermute only.
A program may use at most 320 MiB of HBM per device.

v0:
```python
import jax
import jax.numpy as jnp
from jax import lax
from jax.sharding import PartitionSpec as P

HEADS = 16
HD = 128
WINDOW = 1024


epsilon = 1e-06
big_negative = -1e30


def shifted(value, axis, steps):
    count = lax.axis_size(axis)
    initial, last = (max(0, -steps), min(count, count - steps))
    return lax.ppermute(value, axis, [(source, source + steps) for source in range(initial, last)])


def rms_scale(values, gain):
    return values * lax.rsqrt(jnp.mean(values * values, axis=-1, keepdims=True) + epsilon) * gain


def rotate(values, place, sign):
    half_width = values.shape[-1] // 2
    frequency = 10000.0 ** (-jnp.arange(half_width, dtype=jnp.float32) / half_width)
    angle = place.astype(jnp.float32)[..., None] * frequency
    cosine = jnp.cos(angle)
    sine = sign * jnp.sin(angle)
    first = values[..., :half_width]
    second = values[..., half_width:]
    return jnp.concatenate(
        [first * cosine - second * sine, first * sine + second * cosine], axis=-1
    )


def layout(lengths, packing, positions):
    slots = jnp.arange(lengths.shape[0], dtype=jnp.int32)
    picked = (packing[:, None] == slots[None, :]).astype(jnp.int32)
    packed = jnp.sum(picked * lengths[None, :], axis=1, dtype=jnp.int32)
    ends = jnp.cumsum(packed, dtype=jnp.int32)
    starts = ends - packed
    segment = jnp.sum(
        (positions[:, None] >= ends[None, :]).astype(jnp.int32), axis=1, dtype=jnp.int32
    )
    begin = jnp.sum(
        jnp.where(segment[:, None] == slots[None, :], starts[None, :], 0), axis=1, dtype=jnp.int32
    )
    segment = jnp.where(positions < 0, -1, segment)
    return (segment, positions - begin)


def matmul(left, right):
    return jnp.dot(left, right, preferred_element_type=jnp.float32)


def inner_rows(left, right):
    return lax.dot_general(
        left, right, (((0,), (0,)), ((), ())), preferred_element_type=jnp.float32
    )


def inner_cols(left, right):
    return lax.dot_general(
        left, right, (((1,), (1,)), ((), ())), preferred_element_type=jnp.float32
    )


def gated(gate_values, upper_values):
    return jax.nn.gelu(gate_values) * upper_values


def shards(
    tokens,
    seq_lengths,
    seq_order,
    norm_gain,
    query_weight,
    key_value_weight,
    out_weight,
    mlp_gain,
    gate_weight,
    up_weight,
    down_weight,
    cotangent,
):
    row_count = tokens.shape[2]
    width = tokens.shape[3]
    seq_count = lax.axis_size("seq")
    group_rows = row_count * seq_count
    head_count = HEADS
    local_heads = head_count // seq_count
    head_dim = HD
    score_scale = head_dim ** (-0.5)
    block_count = group_rows // group_rows
    reach_count = -(-WINDOW // group_rows)
    shard_index = lax.axis_index("shard")
    seq_index = lax.axis_index("seq")
    lengths = seq_lengths[0]
    packing = seq_order[0]
    group_start = shard_index * group_rows
    token_index = group_start + seq_index * row_count + jnp.arange(row_count, dtype=jnp.int32)
    token_segment, token_place = layout(lengths, packing, token_index)
    query_index = group_start + jnp.arange(group_rows, dtype=jnp.int32)
    query_segment, query_place = layout(lengths, packing, query_index)
    key_index = group_start - WINDOW + jnp.arange(WINDOW + group_rows, dtype=jnp.int32)
    key_segment, key_place = layout(lengths, packing, key_index)
    weights = (
        lax.all_gather(norm_gain, ("seq", "shard"), axis=0, tiled=True),
        lax.all_gather(query_weight, ("seq", "shard"), axis=0, tiled=True),
        lax.all_gather(key_value_weight, ("seq", "shard"), axis=0, tiled=True),
        lax.all_gather(out_weight, ("seq", "shard"), axis=0, tiled=True),
        lax.all_gather(mlp_gain, ("seq", "shard"), axis=0, tiled=True),
        lax.all_gather(gate_weight, ("seq", "shard"), axis=0, tiled=True),
        lax.all_gather(up_weight, ("seq", "shard"), axis=0, tiled=True),
        lax.all_gather(down_weight, ("seq", "shard"), axis=0, tiled=True),
    )
    gain_one, w_query, w_pair, w_out, gain_two, w_gate, w_upper, w_down = weights
    gain_one = gain_one.astype(jnp.float32)
    gain_two = gain_two.astype(jnp.float32)
    inputs = tokens[0, 0].astype(jnp.float32)
    normed_one = rms_scale(inputs, gain_one).astype(jnp.bfloat16)
    query_pre = matmul(normed_one, w_query)
    queries_local = rotate(
        query_pre.reshape(row_count, head_count, head_dim), token_place[:, None], 1.0
    )
    queries_local = queries_local.astype(jnp.bfloat16).reshape(row_count, width)
    pair_pre = matmul(normed_one, w_pair)
    keys_rotated = rotate(pair_pre[:, :head_dim], token_place, 1.0)
    pair_local = jnp.concatenate([keys_rotated, pair_pre[:, head_dim:]], axis=1).astype(
        jnp.bfloat16
    )
    query_heads = lax.all_to_all(queries_local, "seq", split_axis=1, concat_axis=0, tiled=True)
    pair_group = lax.all_gather(pair_local, "seq", axis=0, tiled=True)
    earlier = []
    current = pair_group
    for section in range(reach_count):
        current = shifted(current, "shard", 1)
        earlier = [current] + earlier
    key_table = jnp.concatenate(earlier + [pair_group], axis=0)
    queries = query_heads.reshape(group_rows, local_heads, head_dim)

    def block_scores():
        raw = jnp.einsum(
            "qhd,kd->hqk", queries, key_table[:, :head_dim], preferred_element_type=jnp.float32
        )
        scores = raw * score_scale
        distance = query_index[:, None] - key_index[None, :]
        allowed = (
            (query_segment[:, None] == key_segment[None, :]) & (distance >= 0) & (distance < WINDOW)
        )
        return (jnp.where(allowed[None], scores, big_negative), queries, key_table)

    def forward_block(number):
        scores, query_block, key_block = block_scores()
        top_score = jnp.max(scores, axis=-1, keepdims=True)
        expo = jnp.exp(scores - top_score)
        row_total = jnp.sum(expo, axis=-1, keepdims=True)
        soft = (expo / row_total).astype(jnp.bfloat16)
        attended = jnp.einsum(
            "hqk,kd->qhd", soft, key_block[:, head_dim:], preferred_element_type=jnp.float32
        )
        return (attended.astype(jnp.bfloat16), (top_score + jnp.log(row_total))[..., 0])

    attended_blocks, log_total = lax.map(forward_block, jnp.arange(block_count, dtype=jnp.int32))
    attended_heads = attended_blocks.reshape(group_rows, local_heads * head_dim)
    merged = lax.all_to_all(attended_heads, "seq", split_axis=0, concat_axis=1, tiled=True)
    middle = inputs + matmul(merged, w_out)
    normed_two = rms_scale(middle, gain_two).astype(jnp.bfloat16)
    gate_values = matmul(normed_two, w_gate)
    upper_values = matmul(normed_two, w_upper)
    hidden = gated(gate_values, upper_values).astype(jnp.bfloat16)
    result = middle + matmul(hidden, w_down)
    layer_output = result.astype(jnp.bfloat16)[None, None]
    weights = (
        lax.all_gather(norm_gain, ("seq", "shard"), axis=0, tiled=True),
        lax.all_gather(query_weight, ("seq", "shard"), axis=0, tiled=True),
        lax.all_gather(key_value_weight, ("seq", "shard"), axis=0, tiled=True),
        lax.all_gather(out_weight, ("seq", "shard"), axis=0, tiled=True),
        lax.all_gather(mlp_gain, ("seq", "shard"), axis=0, tiled=True),
        lax.all_gather(gate_weight, ("seq", "shard"), axis=0, tiled=True),
        lax.all_gather(up_weight, ("seq", "shard"), axis=0, tiled=True),
        lax.all_gather(down_weight, ("seq", "shard"), axis=0, tiled=True),
    )
    gain_one, w_query, w_pair, w_out, gain_two, w_gate, w_upper, w_down = weights
    gain_one = gain_one.astype(jnp.float32)
    gain_two = gain_two.astype(jnp.float32)
    grad_output = cotangent[0, 0]
    grad_down = inner_rows(hidden, grad_output)
    grad_hidden = inner_cols(grad_output, w_down)
    gated_value, gated_back = jax.vjp(gated, gate_values, upper_values)
    grad_gate, grad_upper = gated_back(grad_hidden)
    grad_gate = grad_gate.astype(jnp.bfloat16)
    grad_upper = grad_upper.astype(jnp.bfloat16)
    grad_wgate = inner_rows(normed_two, grad_gate)
    grad_wupper = inner_rows(normed_two, grad_upper)
    grad_normed_two = inner_cols(grad_gate, w_gate) + inner_cols(grad_upper, w_upper)
    norm_value, second_back = jax.vjp(rms_scale, middle, gain_two)
    grad_middle_add, grad_gain_two = second_back(grad_normed_two)
    grad_middle = grad_output.astype(jnp.float32) + grad_middle_add
    grad_branch = grad_middle.astype(jnp.bfloat16)
    grad_wout = inner_rows(merged, grad_branch)
    grad_merged = inner_cols(grad_branch, w_out).astype(jnp.bfloat16)
    grad_heads = lax.all_to_all(
        grad_merged, "seq", split_axis=1, concat_axis=0, tiled=True
    ).reshape(group_rows, local_heads, head_dim)

    def backward_block(carried, number):
        scores, query_block, key_block = block_scores()
        lse = lax.dynamic_index_in_dim(log_total, number, 0, keepdims=False)
        soft = jnp.exp(scores - lse[..., None])
        grad_soft = jnp.einsum(
            "qhd,kd->hqk", grad_heads, key_block[:, head_dim:], preferred_element_type=jnp.float32
        )
        grad_values = jnp.einsum(
            "hqk,qhd->kd", soft.astype(jnp.bfloat16), grad_heads, preferred_element_type=jnp.float32
        )
        delta = jnp.sum(soft * grad_soft, axis=-1, keepdims=True)
        grad_scores = (soft * (grad_soft - delta)).astype(jnp.bfloat16)
        grad_query = (
            jnp.einsum(
                "hqk,kd->qhd",
                grad_scores,
                key_block[:, :head_dim],
                preferred_element_type=jnp.float32,
            )
            * score_scale
        )
        grad_keys = (
            jnp.einsum("hqk,qhd->kd", grad_scores, query_block, preferred_element_type=jnp.float32)
            * score_scale
        )
        update = jnp.concatenate([grad_keys, grad_values], axis=1)
        window_part = carried + update
        carried = window_part
        return (carried, grad_query)

    pair_grads, query_grads = lax.scan(
        backward_block,
        jnp.zeros((WINDOW + group_rows, 2 * head_dim), jnp.float32),
        jnp.arange(block_count, dtype=jnp.int32),
    )
    query_grads = query_grads.reshape(group_rows, local_heads, head_dim)
    query_back = (
        rotate(query_grads, query_place[:, None], -1.0)
        .astype(jnp.bfloat16)
        .reshape(group_rows, local_heads * head_dim)
    )
    query_tokens = lax.all_to_all(query_back, "seq", split_axis=0, concat_axis=1, tiled=True)
    padded = jnp.concatenate(
        [
            jnp.zeros((reach_count * group_rows - WINDOW, 2 * head_dim), jnp.float32),
            pair_grads[:WINDOW],
        ],
        axis=0,
    )
    returned = padded[:group_rows]
    for section in range(1, reach_count + 1):
        returned = shifted(returned.astype(jnp.bfloat16), "shard", -1).astype(returned.dtype)
        if section < reach_count:
            returned = returned + padded[section * group_rows : (section + 1) * group_rows]
    group_grads = pair_grads[WINDOW:] + returned
    own_grads = lax.psum_scatter(
        group_grads.astype(jnp.bfloat16), "seq", scatter_dimension=0, tiled=True
    ).astype(jnp.float32)
    keys_back = rotate(own_grads[:, :head_dim], token_place, -1.0)
    pair_back = jnp.concatenate([keys_back, own_grads[:, head_dim:]], axis=1).astype(jnp.bfloat16)
    grad_wquery = inner_rows(normed_one, query_tokens)
    grad_wpair = inner_rows(normed_one, pair_back)
    grad_normed_one = inner_cols(query_tokens, w_query) + inner_cols(pair_back, w_pair)
    first_value, first_back = jax.vjp(rms_scale, inputs, gain_one)
    grad_inputs_add, grad_gain_one = first_back(grad_normed_one)
    input_grad = (grad_middle + grad_inputs_add)[None, None]
    grads = (
        grad_gain_one,
        grad_wquery,
        grad_wpair,
        grad_wout,
        grad_gain_two,
        grad_wgate,
        grad_wupper,
        grad_down,
    )
    shares = (
        lax.psum_scatter(
            grads[0].astype(jnp.bfloat16), ("seq", "shard"), scatter_dimension=0, tiled=True
        ).astype(jnp.float32),
        lax.psum_scatter(
            grads[1].astype(jnp.bfloat16), ("seq", "shard"), scatter_dimension=0, tiled=True
        ).astype(jnp.float32),
        lax.psum_scatter(
            grads[2].astype(jnp.bfloat16), ("seq", "shard"), scatter_dimension=0, tiled=True
        ).astype(jnp.float32),
        lax.psum_scatter(
            grads[3].astype(jnp.bfloat16), ("seq", "shard"), scatter_dimension=0, tiled=True
        ).astype(jnp.float32),
        lax.psum_scatter(
            grads[4].astype(jnp.bfloat16), ("seq", "shard"), scatter_dimension=0, tiled=True
        ).astype(jnp.float32),
        lax.psum_scatter(
            grads[5].astype(jnp.bfloat16), ("seq", "shard"), scatter_dimension=0, tiled=True
        ).astype(jnp.float32),
        lax.psum_scatter(
            grads[6].astype(jnp.bfloat16), ("seq", "shard"), scatter_dimension=0, tiled=True
        ).astype(jnp.float32),
        lax.psum_scatter(
            grads[7].astype(jnp.bfloat16), ("seq", "shard"), scatter_dimension=0, tiled=True
        ).astype(jnp.float32),
    )
    totals = (
        lax.psum(shares[0].astype(jnp.bfloat16), "grp").astype(jnp.float32),
        lax.psum(shares[1].astype(jnp.bfloat16), "grp").astype(jnp.float32),
        lax.psum(shares[2].astype(jnp.bfloat16), "grp").astype(jnp.float32),
        lax.psum(shares[3].astype(jnp.bfloat16), "grp").astype(jnp.float32),
        lax.psum(shares[4].astype(jnp.bfloat16), "grp").astype(jnp.float32),
        lax.psum(shares[5].astype(jnp.bfloat16), "grp").astype(jnp.float32),
        lax.psum(shares[6].astype(jnp.bfloat16), "grp").astype(jnp.float32),
        lax.psum(shares[7].astype(jnp.bfloat16), "grp").astype(jnp.float32),
    )
    return (
        layer_output,
        input_grad,
        totals[0],
        totals[1],
        totals[2],
        totals[3],
        totals[4],
        totals[5],
        totals[6],
        totals[7],
    )


def solution(mesh):
    return jax.shard_map(
        shards,
        mesh=mesh,
        in_specs=(
            P("grp", "shard", "seq", None),
            P("grp", None),
            P("grp", None),
            P(("seq", "shard")),
            P(("seq", "shard"), None),
            P(("seq", "shard"), None),
            P(("seq", "shard"), None),
            P(("seq", "shard")),
            P(("seq", "shard"), None),
            P(("seq", "shard"), None),
            P(("seq", "shard"), None),
            P("grp", "shard", "seq", None),
        ),
        out_specs=(
            P("grp", "shard", "seq", None),
            P("grp", "shard", "seq", None),
            P(("seq", "shard")),
            P(("seq", "shard"), None),
            P(("seq", "shard"), None),
            P(("seq", "shard"), None),
            P(("seq", "shard")),
            P(("seq", "shard"), None),
            P(("seq", "shard"), None),
            P(("seq", "shard"), None),
        ),
        check_vma=False,
    )
```

profile of v0, /device:TPU:4, one launch (start us, length us, event | category | flops | bytes accessed | tf_op | source)
XLA Modules:
  0.0 1381.5 jit_solution(8270819249241649312)
XLA Ops:
  14.8 59.3 %all-reduce.5 = (bf16[2048]{0:T(1024)(128)(2,1)S(1)}, bf16[2048]{0:T(1024)(128)(2,1)S(1)}) all-reduce(bf16[2048]{0:T(1024)(128)(2,1)S(1)} %dynamic-update-slice, bf16[2048]{0:T(1024)(128)(2,1)S(1)} %dynamic-update-slice.1), channel_id=1, replica_groups=mesh['seq'=4,'shard'=8,'grp'=4] {'seq','shard'}, use_global_device_ids=true, to_apply=%add | all-reduce | flops 4096 | bytes 16384
  79.8 12.6 all_gather.37
  94.5 11.2 collective-permute-done
  111.0 11.9 copy.115
  135.7 8.6 all-to-all-done
  159.1 10.7 all-gather.11.cloned.1.call-done
  176.3 87.1 %all-gather.13.cloned.1.call-done = bf16[2048,6144]{1,0:T(8,128)(2,1)} async-done(((bf16[64,6144]{1,0:T(8,128)(2,1)}), bf16[2048,6144]{1,0:T(8,128)(2,1)}) %all-gather.13.cloned.1.call-update) | async-done | bytes 25165840 | tf_op jit(solution)/shard_map/all_gather | solution.py:115
  263.4 13.3 fusion.88
  276.7 80.4 %all-gather.15.cloned.1.call-done = bf16[2048,6144]{1,0:T(8,128)(2,1)} async-done(((bf16[64,6144]{1,0:T(8,128)(2,1)}), bf16[2048,6144]{1,0:T(8,128)(2,1)}) %all-gather.15.cloned.1.call-update) | async-done | bytes 25165840 | tf_op jit(solution)/shard_map/all_gather | solution.py:116
  357.1 13.2 fusion.89
  370.3 80.5 %all-gather.17.cloned.1.call-done = bf16[6144,2048]{1,0:T(8,128)(2,1)} async-done(((bf16[192,2048]{1,0:T(8,128)(2,1)}), bf16[6144,2048]{1,0:T(8,128)(2,1)}) %all-gather.17.cloned.1.call-update) | async-done | bytes 25165840 | tf_op jit(solution)/shard_map/all_gather | solution.py:117
  450.8 16.7 %multiply_convert_fusion = (bf16[128,6144]{1,0:T(8,128)(2,1)}, bf16[128,6144]{1,0:T(8,128)(2,1)}, bf16[128,6144]{1,0:T(8,128)(2,1)}) fusion(f32[128,6144]{1,0:T(8,128)} %fusion.88, f32[128,6144]{1,0:T(8,128)} %fusion.89, bf16[6144,2048]{1,0:T(8,128)(2,1)} %all-gather.17.cloned.1.call-done, bf16[1,1,128,2048]{3,2,1,0:T(8,128)(2,1)S(1)} %copy-done.6), kind=kOutput, calls=%fused_computation.30 | convolution fusion | flops 3241672704 | bytes 36700160 | tf_op jit(solution)/shard_map/dot_general | solution.py:65
  467.5 13.9 %fusion.90 = f32[128,2048]{1,0:T(8,128)S(1)} fusion(bf16[128,6144]{1,0:T(8,128)(2,1)} %get-tuple-element.87, bf16[2048,6144]{1,0:T(8,128)(2,1)} %all-gather.13.cloned.1.call-done), kind=kOutput, calls=%fused_computation.164 | convolution fusion | flops 3221225472 | bytes 27787264 | tf_op jit(solution)/shard_map/dot_general | solution.py:65
  481.4 14.5 %multiply_reduce_fusion = (bf16[2048]{0:T(1024)(128)(2,1)S(1)}, f32[128]{0:T(128)S(1)}, f32[128,2048]{1,0:T(8,128)}) fusion(f32[128,2048]{1,0:T(8,128)S(1)} %get-tuple-element.108, f32[128]{0:T(128)S(1)} %fusion.82, f32[2048]{0:T(1024)S(1)} %convert_element_type.215, f32[128,2048]{1,0:T(8,128)S(1)} %fusion.90, bf16[128,6144]{1,0:T(8,128)(2,1)} %get-tuple-element.86, ...), kind=kOutput, calls=%fused_computation.73 | convolution fusion | flops 3223058432 | bytes 29897728 | tf_op jit(solution)/shard_map/dot_general | solution.py:65
  509.1 10.0 all-to-all-done.2
  523.1 7.5 fusion
  530.7 7.0 fusion.18
  562.4 6.6 convolution_convert_fusion.3
  577.8 13.1 all_to_all.64
  597.5 14.3 %convolution_convert_fusion.2 = bf16[2048,6144]{1,0:T(8,128)(2,1)} fusion(bf16[128,2048]{1,0:T(8,128)(2,1)S(1)} %multiply_convert_fusion.2, bf16[128,6144]{1,0:T(8,128)(2,1)} %get-tuple-element.87), kind=kOutput, calls=%fused_computation.2 | convolution fusion | flops 3233808384 | bytes 27262976 | tf_op jit(solution)/shard_map/dot_general | solution.py:59
  611.9 14.2 %convolution_convert_fusion.1 = bf16[2048,6144]{1,0:T(8,128)(2,1)} fusion(bf16[128,2048]{1,0:T(8,128)(2,1)S(1)} %multiply_convert_fusion.2, bf16[128,6144]{1,0:T(8,128)(2,1)} %get-tuple-element.86), kind=kOutput, calls=%fused_computation.1 | convolution fusion | flops 3233808384 | bytes 27262976 | tf_op jit(solution)/shard_map/dot_general | solution.py:59
  627.1 13.6 convolution_convert_fusion
  644.3 35.7 %reduce-scatter.14.cloned.1.call-done = bf16[64,2048]{1,0:T(8,128)(2,1)} async-done(((bf16[2048,2048]{1,0:T(8,128)(2,1)}), bf16[64,2048]{1,0:T(8,128)(2,1)}) %reduce-scatter.14.cloned.1.call-update) | async-done | bytes 262160 | tf_op jit(solution)/shard_map/reduce_scatter | solution.py:295
  680.0 95.8 %reduce-scatter.10.cloned.1.call-done = bf16[64,2048]{1,0:T(8,128)(2,1)} async-done(((bf16[2048,2048]{1,0:T(8,128)(2,1)}), bf16[64,2048]{1,0:T(8,128)(2,1)}) %reduce-scatter.10.cloned.1.call-update) | async-done | bytes 262160 | tf_op jit(solution)/shard_map/reduce_scatter | solution.py:289
  775.8 144.2 %reduce-scatter.16.cloned.1.call-done = bf16[64,6144]{1,0:T(8,128)(2,1)} async-done(((bf16[2048,6144]{1,0:T(8,128)(2,1)}), bf16[64,6144]{1,0:T(8,128)(2,1)}) %reduce-scatter.16.cloned.1.call-update) | async-done | bytes 786448 | tf_op jit(solution)/shard_map/reduce_scatter | solution.py:301
  920.0 143.9 %reduce-scatter.18.cloned.1.call-done = bf16[64,6144]{1,0:T(8,128)(2,1)} async-done(((bf16[2048,6144]{1,0:T(8,128)(2,1)}), bf16[64,6144]{1,0:T(8,128)(2,1)}) %reduce-scatter.18.cloned.1.call-update) | async-done | bytes 786448 | tf_op jit(solution)/shard_map/reduce_scatter | solution.py:304
  1063.9 144.3 %reduce-scatter.20.cloned.1.call-done = bf16[192,2048]{1,0:T(8,128)(2,1)} async-done(((bf16[6144,2048]{1,0:T(8,128)(2,1)}), bf16[192,2048]{1,0:T(8,128)(2,1)}) %reduce-scatter.20.cloned.1.call-update) | async-done | bytes 786448 | tf_op jit(solution)/shard_map/reduce_scatter | solution.py:307
  1208.2 12.9 fusion.23
  1221.1 6.5 fusion.91
  1229.1 56.3 %all-reduce.4 = (bf16[2048]{0:T(1024)(128)(2,1)S(1)}, bf16[2048]{0:T(1024)(128)(2,1)S(1)}) all-reduce(bf16[2048]{0:T(1024)(128)(2,1)S(1)} %get-tuple-element.61, bf16[2048]{0:T(1024)(128)(2,1)S(1)} %get-tuple-element.59), channel_id=3, replica_groups=mesh['seq'=4,'shard'=8,'grp'=4] {'seq','shard'}, use_global_device_ids=true, to_apply=%region_16.17.clone | all-reduce | flops 4096 | bytes 16384
  1289.2 18.2 %all-reduce.6 = (bf16[64]{0:T(256)(128)(2,1)S(1)}, bf16[64,256]{1,0:T(8,128)(2,1)S(1)}, bf16[64]{0:T(256)(128)(2,1)S(1)}) all-reduce(bf16[64]{0:T(256)(128)(2,1)S(1)} %dynamic-slice.3, bf16[64,256]{1,0:T(8,128)(2,1)} %reduce-scatter.12.cloned.1.call-done, ...), channel_id=1, replica_groups=mesh['seq'=4,'shard'=8,'grp'=4] {'grp'}, use_global_device_ids=true, to_apply=%region_17.18 | all-reduce | flops 16512 | bytes 66048 | tf_op jit(solution)/shard_map/psum | solution.py:312
  1309.0 54.8 %all-reduce.10.cloned.1.call-done = (bf16[64,2048]{1,0:T(8,128)(2,1)}, bf16[64,2048]{1,0:T(8,128)(2,1)}, bf16[64,6144]{1,0:T(8,128)(2,1)}, bf16[64,6144]{1,0:T(8,128)(2,1)}, bf16[192,2048]{1,0:T(8,128)(2,1)}) async-done(((bf16[64,2048]{1,0:T(8,128)(2,1)}, bf16[64,2048]{1,0:T(8,128)(2,1)}, bf16[64,6144]{1,0:T(8,128)(2,1)}, bf16[64,6144]{1,0:T(8,128)(2,1)}, bf16[192,2048]{1,0:T(8,128)(2,1)}), ...) | async-done | bytes 2883600 | tf_op jit(solution)/shard_map/psum | solution.py:313
  (172 shorter events, 132.7 us)
Async XLA Ops:
  7.2 70.1 %all-gather.7.cloned.1.call-start = ((), (), s32[]{:S(2)}) async-start(), calls=%async_computation.11 | async-start | bytes 1081344 | tf_op jit(solution)/shard_map/all_gather | solution.py:112
  7.9 103.1 %all-gather.9.cloned.1.call-start = ((), (), s32[]{:S(2)}) async-start(), calls=%async_computation.12 | async-start | bytes 8650752 | tf_op jit(solution)/shard_map/all_gather | solution.py:111
  8.7 161.2 %all-gather.11.cloned.1.call-start = ((), (), s32[]{:S(2)}) async-start(), calls=%async_computation.13 | async-start | bytes 8650752 | tf_op jit(solution)/shard_map/all_gather | solution.py:113
  9.4 254.0 %all-gather.13.cloned.1.call-start = ((), (), s32[]{:S(2)}) async-start(), calls=%async_computation.14 | async-start | bytes 25952256 | tf_op jit(solution)/shard_map/all_gather | solution.py:115
  10.0 347.1 %all-gather.15.cloned.1.call-start = ((), (), s32[]{:S(2)}) async-start(), calls=%async_computation.15 | async-start | bytes 25952256 | tf_op jit(solution)/shard_map/all_gather | solution.py:116
  10.6 440.2 %all-gather.17.cloned.1.call-start = ((), (), s32[]{:S(2)}) async-start(), calls=%async_computation.16 | async-start | bytes 25952256 | tf_op jit(solution)/shard_map/all_gather | solution.py:117
  77.2 17.1 %copy-start.12 = (f32[128]{0:T(128)}, f32[128]{0:T(128)S(1)}, u32[]{:S(2)}) copy-start(f32[128]{0:T(128)S(1)} %subtract_convert_fusion.3) | copy-start | bytes 1540
  92.4 13.2 collective-permute-start
  105.7 29.9 %collective-permute-start.1 = (bf16[512,256]{1,0:T(8,128)(2,1)S(1)}, bf16[512,256]{1,0:T(8,128)(2,1)S(1)}, u32[]{:S(2)}, u32[]{:S(2)}) collective-permute-start(bf16[512,256]{1,0:T(8,128)(2,1)S(1)} %collective-permute-done), channel_id=1, source_target_pairs={{0,4},{4,8},{8,12},{12,16},{16,20},{20,24},{24,28},{1,5},{5,9},{9,... | collective-permute-start | bytes 786440 | tf_op jit(solution)/shard_map/ppermute | solution.py:18
  111.0 11.9 copy-start.1
  130.2 14.1 %all-to-all-start = ((bf16[128,4,512]{2,0,1:T(8,128)(2,1)}), bf16[128,4,512]{2,0,1:T(8,128)(2,1)S(1)}, u32[]{:S(2)}, u32[]{:S(2)}) async-start(bf16[128,4,512]{2,0,1:T(8,128)(2,1)} %copy.116), calls=%async_computation | async-start | bytes 1048576 | tf_op jit(solution)/shard_map/all_to_all | solution.py:134
  135.7 13.2 copy-start.8
  155.4 15.8 %all-to-all-start.1 = ((bf16[4,128,512]{1,2,0:T(8,128)(2,1)}), bf16[4,128,512]{1,2,0:T(8,128)(2,1)S(1)}, u32[]{:S(2)}, u32[]{:S(2)}) async-start(bf16[4,128,512]{1,2,0:T(8,128)(2,1)} %copy.120), calls=%async_computation.1 | async-start | bytes 1048576 | tf_op jit(solution)/shard_map/all_to_all | solution.py:168
  276.7 174.1 %copy-start.6 = (bf16[1,1,128,2048]{3,2,1,0:T(8,128)(2,1)S(1)}, bf16[1,1,128,2048]{3,2,1,0:T(8,128)(2,1)}, u32[]{:S(2)}) copy-start(bf16[1,1,128,2048]{3,2,1,0:T(8,128)(2,1)} %param.23) | copy-start | bytes 1572868
  504.7 14.4 %all-to-all-start.2 = ((bf16[128,4,512]{2,0,1:T(8,128)(2,1)}), bf16[128,4,512]{2,0,1:T(8,128)(2,1)}, u32[]{:S(2)}, u32[]{:S(2)}) async-start(bf16[128,4,512]{2,0,1:T(8,128)(2,1)} %bitcast.155), calls=%async_computation.2 | async-start | bytes 1048576 | tf_op jit(solution)/shard_map/all_to_all | solution.py:205
  508.8 132.0 %reduce-scatter.22.cloned.1.call-start = ((), (), s32[]{:S(2)}) async-start(), calls=%async_computation.23 | async-start | bytes 327680
  523.1 7.5 copy-start.3
  523.1 14.5 %slice-start = ((s8[12582912]{0:T(1024)(128)(4,1)}), s8[4194304]{0:T(1024)(128)(4,1)S(1)}, s32[]{:S(2)}) async-start(s8[12582912]{0:T(1024)(128)(4,1)} %bitcast.145), calls=%async_computation.25 | async-start | bytes 8388608
  523.1 14.5 %slice-start.1 = ((s8[12582912]{0:T(1024)(128)(4,1)}), s8[4194304]{0:T(1024)(128)(4,1)S(1)}, s32[]{:S(2)}) async-start(s8[12582912]{0:T(1024)(128)(4,1)} %bitcast.145), calls=%async_computation.26 | async-start | bytes 8388608
  530.7 7.0 slice-start.2
  547.9 5.8 collective-permute-start.2
  553.7 7.7 collective-permute-start.3
  562.4 117.6 %reduce-scatter.14.cloned.1.call-start = ((), (), s32[]{:S(2)}) async-start(), calls=%async_computation.19 | async-start | bytes 8650752 | tf_op jit(solution)/shard_map/reduce_scatter | solution.py:295
  569.0 206.8 %reduce-scatter.10.cloned.1.call-start = ((), (), s32[]{:S(2)}) async-start(), calls=%async_computation.17 | async-start | bytes 8650752 | tf_op jit(solution)/shard_map/reduce_scatter | solution.py:289
  597.5 322.5 %reduce-scatter.16.cloned.1.call-start = ((), (), s32[]{:S(2)}) async-start(), calls=%async_computation.20 | async-start | bytes 25952256 | tf_op jit(solution)/shard_map/reduce_scatter | solution.py:301
  611.8 452.1 %reduce-scatter.18.cloned.1.call-start = ((), (), s32[]{:S(2)}) async-start(), calls=%async_computation.21 | async-start | bytes 25952256 | tf_op jit(solution)/shard_map/reduce_scatter | solution.py:304
  626.1 582.0 %reduce-scatter.20.cloned.1.call-start = ((), (), s32[]{:S(2)}) async-start(), calls=%async_computation.22 | async-start | bytes 25952256 | tf_op jit(solution)/shard_map/reduce_scatter | solution.py:307
  640.8 648.4 %reduce-scatter.12.cloned.1.call-start = ((), (), s32[]{:S(2)}) async-start(), calls=%async_computation.18 | async-start | bytes 1081344 | tf_op jit(solution)/shard_map/reduce_scatter | solution.py:292
  643.6 720.2 %all-reduce.10.cloned.1.call-start = ((), (), s32[]{:S(2)}) async-start(), calls=%async_computation.24 | async-start | bytes 5767168 | tf_op jit(solution)/shard_map/psum | solution.py:313
  1208.2 12.9 copy-start.5
  1221.1 6.5 copy-start.9
  1221.1 64.5 %copy-start.15 = (f32[128]{0:T(128)S(1)}, f32[128]{0:T(128)}, u32[]{:S(2)}) copy-start(f32[128]{0:T(128)} %copy-done.14) | copy-start | bytes 1540
  (8 other events, 20.6 us)
Sparse Core Ops, SparseCore 0:
  10.3 44.8 all-gather.6
  57.4 53.5 all-gather.8
  113.2 56.5 all-gather.10
  171.9 91.3 all-gather.12
  265.5 91.5 all-gather.14
  359.2 91.5 all-gather.16
  562.5 21.2 reduce-scatter.21
  587.9 92.0 reduce-scatter.13
  683.7 92.0 reduce-scatter.9
  780.1 139.8 reduce-scatter.15
  923.9 139.9 reduce-scatter.17
  1068.2 139.8 reduce-scatter.19
  1212.2 76.9 reduce-scatter.11
  1291.9 71.8 all-reduce.9
where the time goes:
time: 1390 us; the launch traced here: 1380 us
  waiting for transfers between devices  923 us (66%)
  matrix products  196 us (14%)
  blocking collectives  159 us (11%)
  local copies, waits for them, and re-layouts  32.9 us (2%)
  other arithmetic  30.2 us (2%)
  starting transfers between devices  23.5 us (2%)
  between operations  16.3 us (1%)
    reduce_scatter x1, waiting for transfers between devices, shards(): lax.psum_scatter(grads[7].astype(jnp.bfloat16), ('seq', 'shard'), scatter...  144 us
    reduce_scatter x1, waiting for transfers between devices, shards(): lax.psum_scatter(grads[5].astype(jnp.bfloat16), ('seq', 'shard'), scatter...  144 us
    reduce_scatter x1, waiting for transfers between devices, shards(): lax.psum_scatter(grads[6].astype(jnp.bfloat16), ('seq', 'shard'), scatter...  144 us
    unnamed x2, blocking collectives  116 us
    reduce_scatter x1, waiting for transfers between devices, shards(): lax.psum_scatter(grads[1].astype(jnp.bfloat16), ('seq', 'shard'), scatter...  95.8 us
    all_gather x1, waiting for transfers between devices, shards(): lax.all_gather(gate_weight, ('seq', 'shard'), axis=0, tiled=True)  87.1 us
    all_gather x1, waiting for transfers between devices, shards(): lax.all_gather(down_weight, ('seq', 'shard'), axis=0, tiled=True)  80.5 us
    all_gather x1, waiting for transfers between devices, shards(): lax.all_gather(up_weight, ('seq', 'shard'), axis=0, tiled=True)  80.4 us
  transfers between devices with their start and end apart: 21, of which 18 were waited for; matrix products, arithmetic and copies ran while one was open for 12% of the time, Pallas kernels for 0%

commit v1 on v0

v1 whole, which is shorter than its diff:
```python
import functools

import jax
import jax.numpy as jnp
from jax import lax
from jax.experimental import pallas as pl
from jax.experimental.pallas import tpu as pltpu
from jax.sharding import PartitionSpec as P

HEADS = 16
HD = 128
WINDOW = 1024
RING = 4
BLOCK = 128
CHUNK = 32
FBLOCK = 512

epsilon = 1e-06
big_negative = -1e30


def send(value, axis, steps):
    count = lax.axis_size(axis)
    return lax.ppermute(value, axis, [(i, (i + steps) % count) for i in range(count)])


def send_x(value, steps):
    return lax.ppermute(
        value,
        "shard",
        [(x * 2 + c, (x + steps) % RING * 2 + c) for x in range(RING) for c in range(2)],
    )


def send_core(value):
    return lax.ppermute(
        value, "shard", [(x * 2 + c, x * 2 + 1 - c) for x in range(RING) for c in range(2)]
    )


def fence(*values):
    return lax.optimization_barrier(values)


def shifted(value, axis, steps):
    count = lax.axis_size(axis)
    initial, last = (max(0, -steps), min(count, count - steps))
    return lax.ppermute(value, axis, [(i, i + steps) for i in range(initial, last)])


def gather_ring(piece, axis):
    half = piece.shape[0] // 2
    after = send(piece, axis, -1)
    before = send(piece, axis, 1)
    far_a = send(after[:half], axis, -1)
    far_b = send(before[half:], axis, 1)
    return [piece, after, jnp.concatenate([far_a, far_b], axis=0), before]


def scatter_ring(parts, axis):
    own, nxt, far, prv = parts
    half = own.shape[0] // 2
    got_a = send(far[:half].astype(jnp.bfloat16), axis, 1).astype(jnp.float32)
    got_b = send(far[half:].astype(jnp.bfloat16), axis, -1).astype(jnp.float32)
    nxt = jnp.concatenate([nxt[:half] + got_a, nxt[half:]], axis=0)
    prv = jnp.concatenate([prv[:half], prv[half:] + got_b], axis=0)
    from_prv = send(nxt.astype(jnp.bfloat16), axis, 1).astype(jnp.float32)
    from_nxt = send(prv.astype(jnp.bfloat16), axis, -1).astype(jnp.float32)
    return own + from_prv + from_nxt


def scatter_direct(pick, axis, index):
    got = [send(pick((index + k) % RING).astype(jnp.bfloat16), axis, k) for k in range(1, RING)]
    return pick(index) + sum(one.astype(jnp.float32) for one in got)


def gather_direct(piece, axis, index):
    got = [send(piece, axis, -k) for k in range(1, RING)]
    return ordered([piece] + got, index)


def scatter_x(pick, index):
    parts = [pick((index + k) % RING) for k in range(RING)]
    got = [send_x(parts[k].astype(jnp.bfloat16), k) for k in range(1, RING)]
    return parts[0] + sum(one.astype(jnp.float32) for one in got)


def ordered(parts, index):
    twice = jnp.stack(parts + parts, axis=0)
    return lax.dynamic_slice_in_dim(twice, (RING - index) % RING, RING, 0)


def exchange_parts(pick, axis, index):
    got = [pick((index + k) % RING) for k in range(RING)]
    return [got[0]] + [send(got[k], axis, k) for k in range(1, RING)]


def by_source(got, index):
    return ordered([got[0], got[3], got[2], got[1]], index)


def exchange(pick, axis, index):
    return by_source(exchange_parts(pick, axis, index), index)


def row_blocks(total):
    rows = total.shape[0] // RING
    return [total[i * rows : (i + 1) * rows] for i in range(RING)]


def norm_scale(values):
    return lax.rsqrt(jnp.mean(values * values, axis=-1, keepdims=True) + epsilon)


def norm_back(values, scale, gain, grad):
    scaled = grad * gain
    dot = jnp.mean(scaled * values, axis=-1, keepdims=True)
    return scaled * scale - values * (scale * scale * scale * dot)


def slot_starts(lengths, packing):
    slots = jnp.arange(lengths.shape[0], dtype=jnp.int32)
    picked = (packing[:, None] == slots[None, :]).astype(jnp.int32)
    packed = jnp.sum(picked * lengths[None, :], axis=1, dtype=jnp.int32)
    return jnp.cumsum(packed, dtype=jnp.int32) - packed


def rotation(place):
    half_width = HD // 2
    frequency = 10000.0 ** (-jnp.arange(half_width, dtype=jnp.float32) / half_width)
    angle = place.astype(jnp.float32)[:, None] * frequency
    cosine, sine = jnp.cos(angle), jnp.sin(angle)
    return jnp.concatenate([cosine, cosine], axis=1), jnp.concatenate([-sine, sine], axis=1)


def matmul(left, right):
    return jnp.dot(left, right, preferred_element_type=jnp.float32)


def inner_rows(left, right):
    return lax.dot_general(
        left, right, (((0,), (0,)), ((), ())), preferred_element_type=jnp.float32
    )


def inner_cols(left, right):
    return lax.dot_general(
        left, right, (((1,), (1,)), ((), ())), preferred_element_type=jnp.float32
    )


def tile_mask(info, tile, first_row, rows, reach, group):
    shard, seq = info[0], info[1]
    base = shard * group
    row = lax.broadcasted_iota(jnp.int32, (rows, 1), 0) + first_row
    query = base + (seq + tile) % RING * BLOCK + row
    begin = jnp.zeros_like(query)
    for slot in range(info.shape[0] - 2):
        start = info[2 + slot]
        begin = jnp.where(query >= start, jnp.maximum(begin, start), begin)
    lowest = jnp.maximum(begin, query - (WINDOW - 1))
    lane = lax.broadcasted_iota(jnp.int32, (1, reach), 1)
    block = lane // group
    in_block = lane - block * group
    key = base + (block - (reach // group - 1)) * group
    key = key + (seq + in_block // BLOCK) % RING * BLOCK + in_block % BLOCK
    return (key <= query) & (key >= lowest)


def attend_kernel(info, q_ref, *refs, heads, group):
    kv_refs, (out_ref, lse_ref, scores_ref, soft_ref) = refs[:-4], refs[-4:]
    reach = group * len(kv_refs)
    tile = pl.program_id(0)
    q = jnp.concatenate([q_ref[:, h * HD : (h + 1) * HD] for h in range(heads)], axis=0)
    for b, kv in enumerate(kv_refs):
        scores_ref[:, b * group : (b + 1) * group] = inner_cols(q, kv[:, :HD])
    for part in range(BLOCK // CHUNK):
        mask = tile_mask(info, tile, part * CHUNK, CHUNK, reach, group)
        for h in range(heads):
            at = pl.ds(h * BLOCK + part * CHUNK, CHUNK)
            scores = jnp.where(mask, scores_ref[at, :] * (HD**-0.5), big_negative)
            top = jnp.max(scores, axis=1, keepdims=True)
            expo = jnp.exp(scores - top)
            total = jnp.sum(expo, axis=1, keepdims=True)
            soft_ref[at, :] = (expo * (1.0 / total)).astype(jnp.bfloat16)
            lse_ref[0, at, :] = jnp.broadcast_to(top + jnp.log(total), (CHUNK, HD))
    acc = None
    for b, kv in enumerate(kv_refs):
        term = jnp.dot(soft_ref[:, b * group : (b + 1) * group], kv[:, HD:], preferred_element_type=jnp.float32)
        acc = term if acc is None else acc + term
    for h in range(heads):
        out_ref[:, h * HD : (h + 1) * HD] = acc[h * BLOCK : (h + 1) * BLOCK].astype(jnp.bfloat16)


def attend(info, queries, kvs):
    group, width = queries.shape
    heads = width // HD
    reach = group * len(kvs)
    whole = pl.BlockSpec((group, 2 * HD), lambda i: (0, 0))
    rows = pl.BlockSpec((BLOCK, width), lambda i: (i, 0))
    return pl.pallas_call(
        functools.partial(attend_kernel, heads=heads, group=group),
        grid=(group // BLOCK,),
        in_specs=[pl.BlockSpec(memory_space=pltpu.SMEM), rows] + [whole] * len(kvs),
        out_specs=[rows, pl.BlockSpec((1, heads * BLOCK, HD), lambda i: (i, 0, 0))],
        out_shape=[
            jax.ShapeDtypeStruct((group, width), jnp.bfloat16),
            jax.ShapeDtypeStruct((group // BLOCK, heads * BLOCK, HD), jnp.float32),
        ],
        scratch_shapes=[
            pltpu.VMEM((heads * BLOCK, reach), jnp.float32),
            pltpu.VMEM((heads * BLOCK, reach), jnp.bfloat16),
        ],
        compiler_params=pltpu.CompilerParams(vmem_limit_bytes=40 * 1024 * 1024),
        name="attend",
    )(info, queries, *kvs)


def attend_back_kernel(info, q_ref, do_ref, lse_ref, cos_ref, sin_ref, *refs, heads, group):
    count = len(refs) - 6
    kv_refs, (dq_ref, dkv_ref, scores_ref, dsoft_ref, soft_ref, dscores_ref) = refs[:count], refs[count:]
    reach = group * count
    tile = pl.program_id(0)

    @pl.when(tile == 0)
    def _():
        dkv_ref[...] = jnp.zeros_like(dkv_ref)

    q = jnp.concatenate([q_ref[:, h * HD : (h + 1) * HD] for h in range(heads)], axis=0)
    do = jnp.concatenate([do_ref[:, h * HD : (h + 1) * HD] for h in range(heads)], axis=0)
    for b, kv in enumerate(kv_refs):
        at = slice(b * group, (b + 1) * group)
        scores_ref[:, at] = inner_cols(q, kv[:, :HD])
        dsoft_ref[:, at] = inner_cols(do, kv[:, HD:])
    for part in range(BLOCK // CHUNK):
        mask = tile_mask(info, tile, part * CHUNK, CHUNK, reach, group)
        for h in range(heads):
            at = pl.ds(h * BLOCK + part * CHUNK, CHUNK)
            lse = lse_ref[0, at, 0:1]
            scores = jnp.where(mask, scores_ref[at, :] * (HD**-0.5), big_negative)
            soft = jnp.exp(scores - lse)
            dsoft = dsoft_ref[at, :]
            delta = jnp.sum(soft * dsoft, axis=1, keepdims=True)
            soft_ref[at, :] = soft.astype(jnp.bfloat16)
            dscores_ref[at, :] = (soft * (dsoft - delta)).astype(jnp.bfloat16)
    dq = None
    for b, kv in enumerate(kv_refs):
        at = slice(b * group, (b + 1) * group)
        term = jnp.dot(dscores_ref[:, at], kv[:, :HD], preferred_element_type=jnp.float32)
        dq = term if dq is None else dq + term
        dkv_ref[b, :, :HD] += inner_rows(dscores_ref[:, at], q) * (HD**-0.5)
        dkv_ref[b, :, HD:] += inner_rows(soft_ref[:, at], do)
    cos, sin = cos_ref[...], sin_ref[...]
    for h in range(heads):
        one = dq[h * BLOCK : (h + 1) * BLOCK] * (HD**-0.5)
        one = one * cos - pltpu.roll(one, HD // 2, 1) * sin
        dq_ref[:, h * HD : (h + 1) * HD] = one.astype(jnp.bfloat16)


def attend_back(info, queries, grads, lse, cos, sin, kvs):
    group, width = queries.shape
    heads = width // HD
    reach = group * len(kvs)
    whole = pl.BlockSpec((group, 2 * HD), lambda i: (0, 0))
    rows = pl.BlockSpec((BLOCK, width), lambda i: (i, 0))
    table = pl.BlockSpec((BLOCK, HD), lambda i: (i, 0))
    return pl.pallas_call(
        functools.partial(attend_back_kernel, heads=heads, group=group),
        grid=(group // BLOCK,),
        in_specs=[
            pl.BlockSpec(memory_space=pltpu.SMEM),
            rows,
            rows,
            pl.BlockSpec((1, heads * BLOCK, HD), lambda i: (i, 0, 0)),
            table,
            table,
        ]
        + [whole] * len(kvs),
        out_specs=[rows, pl.BlockSpec((len(kvs), group, 2 * HD), lambda i: (0, 0, 0))],
        out_shape=[
            jax.ShapeDtypeStruct((group, width), jnp.bfloat16),
            jax.ShapeDtypeStruct((len(kvs), group, 2 * HD), jnp.float32),
        ],
        scratch_shapes=[
            pltpu.VMEM((heads * BLOCK, reach), jnp.float32),
            pltpu.VMEM((heads * BLOCK, reach), jnp.float32),
            pltpu.VMEM((heads * BLOCK, reach), jnp.bfloat16),
            pltpu.VMEM((heads * BLOCK, reach), jnp.bfloat16),
        ],
        compiler_params=pltpu.CompilerParams(vmem_limit_bytes=40 * 1024 * 1024),
        name="attend_back",
    )(info, queries, grads, lse, cos, sin, *kvs)


def project_kernel(
    info, tok_ref, cos_ref, sin_ref, own, after, far_a, far_b, before, near, far,
    n_ref, q_ref, kv_ref, gains_ref, w_ref, sems, *, heads, block
):
    q_cols = heads * HD

    @pl.when(pl.program_id(0) == 0)
    def _():
        x, core = info[0] // 2, info[0] % 2
        copies = []

        def fetch(piece, k, other, first):
            place = (x + k) % RING * 2 + (1 - core if other else core)
            for i in range(piece.shape[0]):
                at = pl.multiple_of((first + i) * 8 * block + place * block, block)
                copies.append(
                    pltpu.make_async_copy(
                        piece.at[i], w_ref.at[pl.ds(at, block), :], sems.at[len(copies)]
                    )
                )

        half = RING // 2
        fetch(own, 0, False, 0)
        fetch(after, 1, False, 0)
        fetch(far_a, 2, False, 0)
        fetch(far_b, 2, False, half)
        fetch(before, 3, False, 0)
        fetch(near.at[0], 0, True, 0)
        fetch(near.at[1], 1, True, 0)
        fetch(far, 2, True, 0)
        fetch(near.at[2], 3, True, 0)
        for copy in copies:
            copy.start()
        for copy in copies:
            copy.wait()
        pick = lax.broadcasted_iota(jnp.int32, (8, HD), 0) == lax.broadcasted_iota(
            jnp.int32, (8, HD), 1
        )
        gains_ref[...] = inner_cols(pick.astype(jnp.bfloat16), w_ref[:, q_cols + 2 * HD :])

    x = tok_ref[...].astype(jnp.float32)
    scale = lax.rsqrt(jnp.mean(x * x, axis=1, keepdims=True) + epsilon)
    normed = (x * scale * gains_ref[0:1, :]).astype(jnp.bfloat16)
    n_ref[...] = normed
    qkv = jnp.dot(normed, w_ref[:, : q_cols + 2 * HD], preferred_element_type=jnp.float32)
    cos, sin = cos_ref[...], sin_ref[...]
    for h in range(heads + 1):
        one = qkv[:, h * HD : (h + 1) * HD]
        one = (one * cos + pltpu.roll(one, HD // 2, 1) * sin).astype(jnp.bfloat16)
        if h < heads:
            q_ref[:, h * HD : (h + 1) * HD] = one
        else:
            kv_ref[:, :HD] = one
    kv_ref[:, HD:] = qkv[:, (heads + 1) * HD :].astype(jnp.bfloat16)


def project(info, tokens, cos, sin, pieces):
    group, width = tokens.shape
    block, columns = pieces[0].shape[1:]
    heads = columns // HD - 3
    rows = lambda n: pl.BlockSpec((BLOCK, n), lambda i: (i, 0))
    whole = lambda shape: pl.BlockSpec(shape, lambda i: (0, 0))
    return pl.pallas_call(
        functools.partial(project_kernel, heads=heads, block=block),
        grid=(group // BLOCK,),
        in_specs=[pl.BlockSpec(memory_space=pltpu.SMEM), rows(width), rows(HD), rows(HD)]
        + [pl.BlockSpec(memory_space=pl.ANY)] * len(pieces),
        out_specs=[
            rows(width),
            rows(heads * HD),
            rows(2 * HD),
            whole((8, width)),
            whole((width, columns)),
        ],
        out_shape=[
            jax.ShapeDtypeStruct((group, width), jnp.bfloat16),
            jax.ShapeDtypeStruct((group, heads * HD), jnp.bfloat16),
            jax.ShapeDtypeStruct((group, 2 * HD), jnp.bfloat16),
            jax.ShapeDtypeStruct((8, width), jnp.float32),
            jax.ShapeDtypeStruct((width, columns), jnp.bfloat16),
        ],
        scratch_shapes=[pltpu.SemaphoreType.DMA((8 * RING,))],
        compiler_params=pltpu.CompilerParams(vmem_limit_bytes=40 * 1024 * 1024),
        name="project",
    )(info, tokens, cos, sin, *pieces)


def feed_kernel(n_ref, gh_ref, gate_ref, up_ref, hidden_ref, grad_ref, back_ref):
    step = pl.program_id(0)
    size = gate_ref.shape[1]
    inner = grad_ref.shape[1] // 2
    gate = jnp.dot(n_ref[...], gate_ref[...], preferred_element_type=jnp.float32)
    upper = jnp.dot(n_ref[...], up_ref[...], preferred_element_type=jnp.float32)
    grad_hidden = gh_ref[...]
    root, cube = 0.7978845608028654, 0.044715
    square = gate * gate
    bend = jnp.tanh(root * gate * (1.0 + cube * square))
    half = 0.5 * (1.0 + bend)
    act = gate * half
    slope = half + 0.5 * gate * (1.0 - bend * bend) * (root * (1.0 + 3.0 * cube * square))
    hidden_ref[...] = (act * upper).astype(jnp.bfloat16)
    grad_gate = (grad_hidden * upper * slope).astype(jnp.bfloat16)
    grad_upper = (grad_hidden * act).astype(jnp.bfloat16)
    grad_ref[:, pl.ds(pl.multiple_of(step * size, size), size)] = grad_gate
    grad_ref[:, pl.ds(pl.multiple_of(inner + step * size, size), size)] = grad_upper
    back = inner_cols(grad_gate, gate_ref[...]) + inner_cols(grad_upper, up_ref[...])

    @pl.when(step == 0)
    def _():
        back_ref[...] = back

    @pl.when(step > 0)
    def _():
        back_ref[...] += back


def feed(normed, grad_hidden, weights):
    group, width = normed.shape
    inner = grad_hidden.shape[1]
    steps = inner // FBLOCK
    whole = lambda n: pl.BlockSpec((group, n), lambda i: (0, 0))
    columns = pl.BlockSpec((group, FBLOCK), lambda i: (0, i))
    return pl.pallas_call(
        feed_kernel,
        grid=(steps,),
        in_specs=[
            whole(width),
            columns,
            pl.BlockSpec((width, FBLOCK), lambda i: (0, i)),
            pl.BlockSpec((width, FBLOCK), lambda i: (0, steps + i)),
        ],
        out_specs=[columns, whole(2 * inner), whole(width)],
        out_shape=[
            jax.ShapeDtypeStruct((group, inner), jnp.bfloat16),
            jax.ShapeDtypeStruct((group, 2 * inner), jnp.bfloat16),
            jax.ShapeDtypeStruct((group, width), jnp.float32),
        ],
        compiler_params=pltpu.CompilerParams(vmem_limit_bytes=56 * 1024 * 1024),
        cost_estimate=pl.CostEstimate(
            flops=8 * group * width * inner,
            bytes_accessed=4 * width * inner,
            transcendentals=group * inner,
        ),
        name="feed",
    )(normed, grad_hidden, weights, weights)


def shards(
    tokens,
    seq_lengths,
    seq_order,
    norm_gain,
    query_weight,
    key_value_weight,
    out_weight,
    mlp_gain,
    gate_weight,
    up_weight,
    down_weight,
    cotangent,
):
    rows = tokens.shape[2]
    width = tokens.shape[3]
    group_rows = rows * RING
    q_cols = HEADS // RING * HD
    f_cols = gate_weight.shape[1] // RING
    own_rows = query_weight.shape[0]
    shard_index = lax.axis_index("shard")
    seq_index = lax.axis_index("seq")
    grp_index = lax.axis_index("grp")
    own_tokens = tokens[0, 0]
    own_cotangent = cotangent[0, 0]

    gains = jnp.pad(jnp.stack([norm_gain, mlp_gain], axis=1), ((0, 0), (0, HD - 2)))

    def pick_q(i):
        own = lax.dynamic_slice_in_dim(query_weight, i * q_cols, q_cols, 1)
        return jnp.concatenate([own, key_value_weight, gains], axis=1)

    def pick_f(i):
        return jnp.concatenate(
            [
                lax.dynamic_slice_in_dim(gate_weight, i * f_cols, f_cols, 1),
                lax.dynamic_slice_in_dim(up_weight, i * f_cols, f_cols, 1),
            ],
            axis=1,
        )

    group_start = shard_index * group_rows
    ring_rows = (seq_index + jnp.arange(RING, dtype=jnp.int32)) % RING * rows
    in_group = (ring_rows[:, None] + jnp.arange(rows, dtype=jnp.int32)[None, :]).reshape(-1)
    query_index = group_start + in_group
    starts = slot_starts(seq_lengths[0], seq_order[0])
    begins = jnp.max(
        jnp.where(query_index[:, None] >= starts[None, :], starts[None, :], 0), axis=1
    )
    cos, sin = rotation(query_index - begins)
    info = jnp.concatenate([jnp.stack([shard_index, seq_index]).astype(jnp.int32), starts])

    def scattered(grad, dim):
        return lax.psum_scatter(grad, "shard", scatter_dimension=dim, tiled=True)

    w_out = lax.all_gather(out_weight, "shard", axis=0, tiled=True)
    got = exchange_parts(pick_q, "seq", seq_index)
    tok_after = send(own_tokens, "seq", -1)
    tok_before = send(own_tokens, "seq", 1)
    *got, tok_after, tok_before, gate_weight, up_weight, down_weight = fence(
        *got, tok_after, tok_before, gate_weight, up_weight, down_weight
    )
    w_down = lax.all_gather(down_weight, "shard", axis=0, tiled=True)
    block = by_source(got, seq_index)
    block_after = send_x(block, -1)
    block_before = send_x(block, 1)
    half = rows // 2
    tok_far_a = send(tok_after[:half], "seq", -1)
    tok_far_b = send(tok_before[half:], "seq", 1)
    block_after, block_before, tok_far_a, tok_far_b, gate_weight, up_weight, w_out = fence(
        block_after, block_before, tok_far_a, tok_far_b, gate_weight, up_weight, w_out
    )
    block_far_a = send_x(block_after[: RING // 2], -1)
    block_far_b = send_x(block_before[RING // 2 :], 1)
    near = send_core(jnp.stack([block, block_after, block_before]))
    got = exchange_parts(pick_f, "seq", seq_index)
    block_far_a, block_far_b, near = fence(block_far_a, block_far_b, near)
    far = send_core(jnp.concatenate([block_far_a, block_far_b]))
    tokens_bf = jnp.concatenate([own_tokens, tok_after, tok_far_a, tok_far_b, tok_before], axis=0)
    pieces = (block, block_after, block_far_a, block_far_b, block_before, near, far)
    normed_one, queries, pair, gain_rows, w_attn = project(info, tokens_bf, cos, sin, pieces)
    *got, own_cotangent, pair = fence(*got, own_cotangent, pair)
    w_ff = lax.all_gather(by_source(got, seq_index), "shard", axis=1, tiled=True)
    w_ff = w_ff.reshape(width, -1)
    gain_one, gain_two = gain_rows[0], gain_rows[1]
    w_qkv = w_attn[:, : q_cols + 2 * HD]
    cot_after = send(own_cotangent, "seq", -1)
    cot_before = send(own_cotangent, "seq", 1)
    kvs = [shifted(pair, "shard", 2), shifted(pair, "shard", 1), pair]
    attended, lse = attend(info, queries, kvs)
    attended, cot_after, cot_before, w_down = fence(attended, cot_after, cot_before, w_down)
    cot_far_a = send(cot_after[:half], "seq", -1)
    cot_far_b = send(cot_before[half:], "seq", 1)
    all_cotangent = jnp.concatenate(
        [own_cotangent, cot_after, cot_far_a, cot_far_b, cot_before], axis=0
    )

    branch = scatter_ring(row_blocks(matmul(attended, w_out)), "seq")
    middle = own_tokens.astype(jnp.float32) + branch
    scale_two = norm_scale(middle)
    normed_two = (middle * scale_two * gain_two).astype(jnp.bfloat16)
    normed_two = jnp.concatenate(gather_ring(normed_two, "seq"), axis=0)
    grad_hidden, normed_two = fence(inner_cols(all_cotangent, w_down), normed_two)
    hidden, grad_ff, partial_two = feed(normed_two, grad_hidden, w_ff)
    grad_wff = inner_rows(normed_two, grad_ff).astype(jnp.bfloat16)
    grad_down = inner_rows(hidden, all_cotangent).astype(jnp.bfloat16)
    share_ff = scattered(grad_wff.reshape(RING, -1, 2 * f_cols), 1)
    grad_normed_two = scatter_ring(row_blocks(partial_two), "seq")
    grad_normed_two, grad_wff, grad_down = fence(grad_normed_two, grad_wff, grad_down)

    x_index, core = shard_index // 2, shard_index % 2
    part = own_rows // RING
    grad_down = grad_down.reshape(RING, 2, RING, -1, width)
    down_other = send_core(lax.dynamic_index_in_dim(grad_down, 1 - core, 1, keepdims=False))
    grad_middle = own_cotangent.astype(jnp.float32) + norm_back(
        middle, scale_two, gain_two, grad_normed_two
    )
    gain_two_terms = (grad_normed_two * middle * scale_two).astype(jnp.bfloat16)
    own_branch = grad_middle.astype(jnp.bfloat16)
    gb_after = send(own_branch, "seq", -1)
    gb_before = send(own_branch, "seq", 1)
    gb_after, gb_before, down_other, grad_down = fence(gb_after, gb_before, down_other, grad_down)
    gb_far_a = send(gb_after[:half], "seq", -1)
    gb_far_b = send(gb_before[half:], "seq", 1)
    mine = lax.dynamic_index_in_dim(grad_down, core, 1, keepdims=False).astype(jnp.float32)
    mine = (mine + down_other.astype(jnp.float32)).astype(jnp.bfloat16)
    down_parts = [
        lax.dynamic_index_in_dim(mine, (grp_index + k) % RING, 1, keepdims=False)
        for k in range(RING)
    ]
    down_a = send(down_parts[2][: RING // 2], "grp", 1)
    down_b = send(down_parts[2][RING // 2 :], "grp", -1)
    gb_far_a, gb_far_b, down_a, down_b, *down_parts = fence(
        gb_far_a, gb_far_b, down_a, down_b, *down_parts
    )
    grad_branch = jnp.concatenate([own_branch, gb_after, gb_far_a, gb_far_b, gb_before], axis=0)
    grad_attended = inner_cols(grad_branch, w_out).astype(jnp.bfloat16)
    down_own, down_next, _, down_last = [one.astype(jnp.float32) for one in down_parts]
    down_next = jnp.concatenate(
        [down_next[: RING // 2] + down_a.astype(jnp.float32), down_next[RING // 2 :]], axis=0
    ).astype(jnp.bfloat16)
    down_last = jnp.concatenate(
        [down_last[: RING // 2], down_last[RING // 2 :] + down_b.astype(jnp.float32)], axis=0
    ).astype(jnp.bfloat16)
    down_next = send(down_next, "grp", 1)
    down_last = send(down_last, "grp", -1)

    grad_queries, grad_table = attend_back(info, queries, grad_attended, lse, cos, sin, kvs)
    grad_wout = inner_rows(attended, grad_branch).astype(jnp.bfloat16)
    grad_queries, grad_table, share_ff, down_next, down_last, grad_wout = fence(
        grad_queries, grad_table, share_ff, down_next, down_last, grad_wout
    )
    share_out = scattered(grad_wout, 0)
    returned_two = shifted(grad_table[0].astype(jnp.bfloat16), "shard", -2)
    returned_one = shifted(grad_table[1].astype(jnp.bfloat16), "shard", -1)
    down_own = down_own + down_next.astype(jnp.float32) + down_last.astype(jnp.float32)
    down_own = scatter_x(
        lambda i: lax.dynamic_index_in_dim(down_own, i, 0, keepdims=False), x_index
    ).astype(jnp.bfloat16)
    returned_one, returned_two, down_own, share_ff, hidden = fence(
        returned_one, returned_two, down_own, share_ff, hidden
    )
    grad_pair = (
        grad_table[2] + returned_one.astype(jnp.float32) + returned_two.astype(jnp.float32)
    )
    grad_keys = grad_pair[:, :HD]
    swapped = jnp.concatenate([grad_keys[:, HD // 2 :], grad_keys[:, : HD // 2]], axis=1)
    grad_keys = grad_keys * cos - swapped * sin
    grad_pair = jnp.concatenate([grad_keys, grad_pair[:, HD:]], axis=1).astype(jnp.bfloat16)
    grad_qkv = jnp.concatenate([grad_queries, grad_pair], axis=1)
    all_tokens = tokens_bf.astype(jnp.float32)
    scale_one = norm_scale(all_tokens)
    partial_one = inner_cols(grad_qkv, w_qkv)
    gain_one_terms = (partial_one * all_tokens * scale_one).astype(jnp.bfloat16)
    columns = jnp.arange(HD)[None, :]
    first_column = jnp.broadcast_to(columns == 0, (group_rows, HD)).astype(jnp.bfloat16)
    second_column = jnp.broadcast_to(columns == 1, (rows, HD)).astype(jnp.bfloat16)
    grad_gains = inner_rows(gain_one_terms, first_column) + inner_rows(
        gain_two_terms, second_column
    )
    grad_attn = jnp.concatenate(
        fence(inner_rows(normed_one, grad_qkv).astype(jnp.bfloat16), grad_gains.astype(jnp.bfloat16)),
        axis=1,
    )

    def spread(share):
        share = share.reshape(RING, RING, part, -1)
        summed = scatter_direct(
            lambda i: lax.dynamic_index_in_dim(share, i, 1, keepdims=False).astype(jnp.float32),
            "grp",
            grp_index,
        )
        return summed.astype(jnp.bfloat16)

    def placed(summed):
        return exchange(
            lambda i: lax.dynamic_index_in_dim(summed, i, 0, keepdims=False), "seq", seq_index
        )

    def side_by_side(columns):
        return columns.transpose(1, 0, 2).reshape(columns.shape[1], -1)

    own_one, next_one, far_one, last_one = row_blocks(partial_one)
    one_a = send(far_one[:half].astype(jnp.bfloat16), "seq", 1)
    one_b = send(far_one[half:].astype(jnp.bfloat16), "seq", -1)
    sum_ff = spread(share_ff)
    one_a, one_b, sum_ff, grad_attn, share_out = fence(one_a, one_b, sum_ff, grad_attn, share_out)
    share_attn = scattered(grad_attn.reshape(RING, -1, grad_attn.shape[1]), 1)
    next_one = jnp.concatenate([next_one[:half] + one_a.astype(jnp.float32), next_one[half:]], axis=0)
    last_one = jnp.concatenate([last_one[:half], last_one[half:] + one_b.astype(jnp.float32)], axis=0)
    from_last = send(next_one.astype(jnp.bfloat16), "seq", 1)
    from_next = send(last_one.astype(jnp.bfloat16), "seq", -1)
    ff_columns = placed(sum_ff)
    from_last, from_next, ff_columns = fence(from_last, from_next, ff_columns)
    grad_normed_one = own_one + from_last.astype(jnp.float32) + from_next.astype(jnp.float32)
    own_inputs = own_tokens.astype(jnp.float32)
    input_grad = grad_middle + norm_back(
        own_inputs, norm_scale(own_inputs), gain_one, grad_normed_one
    )
    ff_rows = jnp.concatenate(
        [
            side_by_side(ff_columns[:, :, :f_cols]),
            side_by_side(ff_columns[:, :, f_cols:]),
            down_own.reshape(part, -1),
        ],
        axis=1,
    )
    ff_after = send(ff_rows, "grp", -1)
    ff_before = send(ff_rows, "grp", 1)
    ff_after, ff_before, share_attn, input_grad = fence(ff_after, ff_before, share_attn, input_grad)
    ff_far_a = send(ff_after[: part // 2], "grp", -1)
    ff_far_b = send(ff_before[part // 2 :], "grp", 1)

    from_out = share_out.reshape(RING, part, RING, -1).transpose(2, 0, 1, 3)
    from_out = from_out.reshape(RING, own_rows, -1)
    summed = spread(jnp.concatenate([share_attn, from_out], axis=2))
    ff_far = jnp.concatenate([ff_far_a, ff_far_b], axis=0)
    summed, ff_far = fence(summed, ff_far)
    ff_rows = ordered([ff_rows, ff_after, ff_far, ff_before], grp_index)
    ff_rows = ff_rows.reshape(own_rows, -1).astype(jnp.float32)
    share_gate = ff_rows[:, : RING * f_cols]
    share_upper = ff_rows[:, RING * f_cols : 2 * RING * f_cols]
    share_down = ff_rows[:, 2 * RING * f_cols :].reshape(-1, width)
    n_attn = share_attn.shape[2]
    out_own = side_by_side(summed[:, :, n_attn:])
    columns = placed(summed[:, :, :n_attn])
    summed = jnp.sum(columns[:, :, q_cols:].astype(jnp.float32), axis=0).astype(jnp.bfloat16)
    attn_rows = jnp.concatenate([side_by_side(columns[:, :, :q_cols]), out_own, summed], axis=1)
    attn_rows = gather_direct(attn_rows, "grp", grp_index).reshape(own_rows, -1)
    attn_rows = attn_rows.astype(jnp.float32)
    share_query = attn_rows[:, :width]
    share_out = attn_rows[:, width : 2 * width]
    share_pair = attn_rows[:, 2 * width : 2 * width + 2 * HD]
    share_gain_one = attn_rows[:, 2 * width + 2 * HD]
    share_gain_two = attn_rows[:, 2 * width + 2 * HD + 1]

    result = middle + scatter_ring(row_blocks(matmul(hidden, w_down)), "seq")
    layer_output = result.astype(jnp.bfloat16)[None, None]
    return (
        layer_output,
        input_grad[None, None],
        share_gain_one,
        share_query,
        share_pair,
        share_out,
        share_gain_two,
        share_gate,
        share_upper,
        share_down,
    )


def solution(mesh):
    by_row = P(("seq", "shard"), None)
    by_entry = P(("seq", "shard"))
    by_token = P("grp", "shard", "seq", None)
    return jax.shard_map(
        shards,
        mesh=mesh,
        in_specs=(
            by_token,
            P("grp", None),
            P("grp", None),
            by_entry,
            by_row,
            by_row,
            by_row,
            by_entry,
            by_row,
            by_row,
            by_row,
            by_token,
        ),
        out_specs=(
            by_token,
            by_token,
            by_entry,
            by_row,
            by_row,
            by_row,
            by_entry,
            by_row,
            by_row,
            by_row,
        ),
        check_vma=False,
    )
```

time: 1390 us -> 488 us (0.35)
  waiting for transfers between devices: 923 us -> 142 us
  blocking collectives: 159 us -> 0 us
  matrix products: 196 us -> 41.4 us
  starting transfers between devices: 23.5 us -> 116 us
  Pallas kernels: 0 us -> 55 us
  local copies, waits for them, and re-layouts: 32.9 us -> 66.1 us
    reduce_scatter x6 -> x3, waiting for transfers between devices: 565 us -> 0.02 us  [scattered(): return lax.psum_scatter(grad, 'shard', scatter_dimension=dim, tiled=True)]
    all_gather x6 -> x3, waiting for transfers between devices: 261 us -> 0.01 us  [the longest x1 0.01 us: shards(): w_out = lax.all_gather(out_weight, 'shard', axis=0, tiled=True)]
    ppermute x4 -> x75, waiting for transfers between devices: 19 us -> 141 us  [the longest x61 117 us: send(): lax.ppermute(value, axis, [(i, (i + steps) % count) for i in range(count)])]
    unnamed x2 -> x0, blocking collectives: 116 us -> none
    ppermute x4 -> x75, starting transfers between devices: 10.6 us -> 116 us  [the longest x61 92.1 us: send(): lax.ppermute(value, axis, [(i, (i + steps) % count) for i in range(count)])]
    pallas_call x0 -> x4, Pallas kernels: none -> 55 us  [the longest x1 22.1 us: feed(): pl.pallas_call(feed_kernel, grid=(steps,), in_specs=[whole(width), column...]
    psum x1 -> x0, waiting for transfers between devices: 54.8 us -> none  [shards(): lax.psum(shares[1].astype(jnp.bfloat16), 'grp').astype(jnp.float32)]
    dot_general x6 -> x3, matrix products: 59.4 us -> 9.14 us  [inner_cols(): lax.dot_general(left, right, (((1,), (1,)), ((), ())), preferred_element_...]
  transfers between devices with their start and end apart: 21 -> 81, of which waited for: 18 -> 34; matrix products, arithmetic and copies ran while one was open for 12% -> 25% of each run, Pallas kernels for 0% -> 7%
where the time goes in v1:
time: 488 us; the launch traced here: 478 us
  waiting for transfers between devices  142 us (29%)
  starting transfers between devices  116 us (24%)
  local copies, waits for them, and re-layouts  66.1 us (14%)
  Pallas kernels  55 us (11%)
  other arithmetic  41.4 us (8%)
  matrix products  41.4 us (8%)
  between operations  16.4 us (3%)
    ppermute x61, waiting for transfers between devices, send(): lax.ppermute(value, axis, [(i, (i + steps) % count) for i in range(count)])  117 us
    ppermute x61, starting transfers between devices, send(): lax.ppermute(value, axis, [(i, (i + steps) % count) for i in range(count)])  92.1 us
    unnamed x199, local copies, waits for them, and re-layouts  33.4 us
    pallas_call x1, Pallas kernels, feed(): pl.pallas_call(feed_kernel, grid=(steps,), in_specs=[whole(width), column...  22.1 us
    dot_general x6, matrix products, inner_rows(): lax.dot_general(left, right, (((0,), (0,)), ((), ())), preferred_element_...  21.4 us
    ppermute x4, waiting for transfers between devices, shifted(): lax.ppermute(value, axis, [(i, i + steps) for i in range(initial, last)])  18.2 us
    ppermute x7, starting transfers between devices, send_x(): lax.ppermute(value, 'shard', [(x * 2 + c, (x + steps) % RING * 2 + c) for...  13.8 us
    pallas_call x1, Pallas kernels, attend_back(): pl.pallas_call(functools.partial(attend_back_kernel, heads=heads, group=g...  12.4 us
  transfers between devices with their start and end apart: 81, of which 34 were waited for; matrix products, arithmetic and copies ran while one was open for 25% of the time, Pallas kernels for 7%

profile of v1, /device:TPU:4, one launch (start us, length us, event | category | flops | bytes accessed | tf_op | source)
XLA Modules:
  0.0 478.2 jit_solution(2717462448884718567)
XLA Ops:
  8.0 4.1 collective-permute-start.3
  23.2 5.3 %collective-permute-done.2 = bf16[64,896]{1,0:T(8,128)(2,1)} collective-permute-done((bf16[64,896]{1,0:T(8,128)(2,1)}, bf16[64,896]{1,0:T(8,128)(2,1)}, u32[]{:S(2)}, u32[]{:S(2)}) %collective-permute-start.2) | collective-permute-done | bytes 114720 | tf_op jit(solution)/shard_map/ppermute | solution.py:24
  55.4 4.7 collective-permute-start.14
  67.8 9.7 %project.1 = (bf16[512,2048]{1,0:T(8,128)(2,1)S(1)}, bf16[512,512]{1,0:T(8,128)(2,1)S(1)}, bf16[512,256]{1,0:T(8,128)(2,1)S(1)}, f32[8,2048]{1,0:T(8,128)S(1)}, bf16[2048,896]{1,0:T(8,128)(2,1)S(1)}) custom-call(s32[8]{0:T(128)S(1)} %pad_add_fusion.info, bf16[512,2048]{1,0:T(8,128)(2,1)S(1)} %constant_dynamic-update-slice_fusion.8.tok_ref, ...), custom_call_target="tpu_custom_call" | custom-call | tf_op jit(solution)/shard_map/project/pallas_call | solution.py:357
  87.6 3.7 collective-permute-start.16
  93.6 5.0 %collective-permute-done.16.refs_0_ = bf16[512,256]{1,0:T(8,128)(2,1)S(1)} collective-permute-done((bf16[512,256]{1,0:T(8,128)(2,1)S(1)}, bf16[512,256]{1,0:T(8,128)(2,1)S(1)}, u32[]{:S(2)}, u32[]{:S(2)}) %collective-permute-start.16) | collective-permute-done | bytes 262176 | tf_op jit(solution)/shard_map/ppermute | solution.py:48
  98.6 10.8 %attend.1 = (bf16[512,512]{1,0:T(8,128)(2,1)S(1)}, f32[4,512,128]{2,1,0:T(8,128)S(1)}) custom-call(s32[8]{0:T(128)S(1)} %pad_add_fusion.info, bf16[512,512]{1,0:T(8,128)(2,1)S(1)} %copy-done.3, bf16[512,256]{1,0:T(8,128)(2,1)S(1)} %collective-permute-done.16.refs_0_, bf16[512,256]{1,0:T(8,128)(2,1)S(1)} %collective-permute-done.17.refs_1_, ...), custom_call_target="tpu_custom_call" | custom-call | tf_op jit(solution)/shard_map/attend/pallas_call | solution.py:201
  118.4 6.4 %collective-permute-done.20 = bf16[64,2048]{1,0:T(8,128)(2,1)S(1)} collective-permute-done((bf16[64,2048]{1,0:T(8,128)(2,1)S(1)}, bf16[64,2048]{1,0:T(8,128)(2,1)S(1)}, u32[]{:S(2)}, u32[]{:S(2)}) %collective-permute-start.20) | collective-permute-done | bytes 262176 | tf_op jit(solution)/shard_map/ppermute | solution.py:24
  134.8 5.6 %collective-permute-done.23 = bf16[128,2048]{1,0:T(8,128)(2,1)S(1)} collective-permute-done((bf16[128,2048]{1,0:T(8,128)(2,1)S(1)}, bf16[128,2048]{1,0:T(8,128)(2,1)S(1)}, u32[]{:S(2)}, u32[]{:S(2)}) %collective-permute-start.23) | collective-permute-done | bytes 524320 | tf_op jit(solution)/shard_map/ppermute | solution.py:24
  140.4 3.8 collective-permute-done.21
  148.0 7.3 %collective-permute-done.26 = bf16[128,2048]{1,0:T(8,128)(2,1)S(1)} collective-permute-done((bf16[128,2048]{1,0:T(8,128)(2,1)S(1)}, bf16[128,2048]{1,0:T(8,128)(2,1)S(1)}, u32[]{:S(2)}, u32[]{:S(2)}) %collective-permute-start.26) | collective-permute-done | bytes 524320 | tf_op jit(solution)/shard_map/ppermute | solution.py:24
  155.3 3.8 collective-permute-start.27
  159.1 5.1 %fusion.72.gh_ref = f32[512,1536]{1,0:T(8,128)} fusion(bf16[512,2048]{1,0:T(8,128)(2,1)S(1)} %constant_dynamic-update-slice_fusion.13, bf16[1536,2048]{1,0:T(8,128)(2,1)S(1)} %bitcast.243), kind=kOutput, calls=%fused_computation.284 | convolution fusion | flops 3221225472 | bytes 11534336 | tf_op jit(solution)/shard_map/dot_general | solution.py:147
  166.3 6.0 %collective-permute-done.29 = bf16[64,2048]{1,0:T(8,128)(2,1)S(1)} collective-permute-done((bf16[64,2048]{1,0:T(8,128)(2,1)S(1)}, bf16[64,2048]{1,0:T(8,128)(2,1)S(1)}, u32[]{:S(2)}, u32[]{:S(2)}) %collective-permute-start.29) | collective-permute-done | bytes 262176 | tf_op jit(solution)/shard_map/ppermute | solution.py:24
  173.9 22.1 %feed.1 = (bf16[512,1536]{1,0:T(8,128)(2,1)}, bf16[512,3072]{1,0:T(8,128)(2,1)}, f32[512,2048]{1,0:T(8,128)}) custom-call(bf16[512,2048]{1,0:T(8,128)(2,1)} %constant_dynamic-update-slice_fusion.18.n_ref, f32[512,1536]{1,0:T(8,128)} %fusion.72.gh_ref, bf16[2048,3072]{1,0:T(8,128)(2,1)} %bitcast.240, bf16[2048,3072]{1,0:T(8,128)(2,1)} %bitcast.241), custom_call_target="tpu_custom_call" | custom-call | flops 12884901888 | bytes 12582912 | tf_op jit(solution)/shard_map/feed/pallas_call | solution.py:417
  196.0 11.8 %convolution_convert_fusion = bf16[2048,3072]{1,0:T(8,128)(2,1)} fusion(bf16[512,2048]{1,0:T(8,128)(2,1)} %constant_dynamic-update-slice_fusion.18.n_ref, bf16[512,3072]{1,0:T(8,128)(2,1)} %get-tuple-element.129), kind=kOutput, calls=%fused_computation | convolution fusion | flops 6448742400 | bytes 17825792 | tf_op jit(solution)/shard_map/dot_general | solution.py:141
  214.6 4.7 collective-permute-done.30
  224.3 3.7 convolution_convert_fusion.1
  230.9 3.8 collective-permute-done.31
  244.2 11.5 %collective-permute-done.35 = bf16[128,2048]{1,0:T(8,128)(2,1)} collective-permute-done((bf16[128,2048]{1,0:T(8,128)(2,1)}, bf16[128,2048]{1,0:T(8,128)(2,1)}, u32[]{:S(2)}, u32[]{:S(2)}) %collective-permute-start.35) | collective-permute-done | bytes 524320 | tf_op jit(solution)/shard_map/ppermute | solution.py:24
  260.9 4.3 fusion
  271.0 6.3 %collective-permute-done.39 = bf16[2,48,2048]{2,1,0:T(8,128)(2,1)S(1)} collective-permute-done((bf16[2,48,2048]{2,1,0:T(8,128)(2,1)S(1)}, bf16[2,48,2048]{2,1,0:T(8,128)(2,1)S(1)}, u32[]{:S(2)}, u32[]{:S(2)}) %collective-permute-start.39) | collective-permute-done | bytes 393248 | tf_op jit(solution)/shard_map/ppermute | solution.py:24
  285.1 12.4 %attend_back.1 = (bf16[512,512]{1,0:T(8,128)(2,1)S(1)}, f32[3,512,256]{2,1,0:T(8,128)S(1)}) custom-call(s32[8]{0:T(128)S(1)} %pad_add_fusion.info, bf16[512,512]{1,0:T(8,128)(2,1)S(1)} %copy-done.3, bf16[512,512]{1,0:T(8,128)(2,1)S(1)} %convolution_convert_fusion.4.do_ref, f32[4,512,128]{2,1,0:T(8,128)S(1)} %copy-done.15, ...), custom_call_target="tpu_custom_call" | custom-call | tf_op jit(solution)/shard_map/attend_back/pallas_call | solution.py:267
  309.8 4.9 %collective-permute-start.46 = (bf16[48,2048]{1,0:T(8,128)(2,1)S(1)}, bf16[48,2048]{1,0:T(8,128)(2,1)S(1)}, u32[]{:S(2)}, u32[]{:S(2)}) collective-permute-start(bf16[48,2048]{1,0:T(8,128)(2,1)S(1)} %get-tuple-element.222), channel_id=1, source_target_pairs={{0,16},{4,20},{8,24},{12,28},{16,0},{20,4},{24,8},{28,12},{1,17},{... | collective-permute-start | bytes 589832 | tf_op jit(solution)/shard_map/ppermute | solution.py:28
  321.1 8.7 %collective-permute-done.44 = bf16[512,256]{1,0:T(8,128)(2,1)S(1)} collective-permute-done((bf16[512,256]{1,0:T(8,128)(2,1)S(1)}, bf16[512,256]{1,0:T(8,128)(2,1)S(1)}, u32[]{:S(2)}, u32[]{:S(2)}) %collective-permute-start.44) | collective-permute-done | bytes 262176 | tf_op jit(solution)/shard_map/ppermute | solution.py:48
  333.8 7.7 %fusion.71 = (bf16[512,2048]{1,0:T(8,128)(2,1)S(1)}, f32[512,2048]{1,0:T(8,128)}) fusion(bf16[512,1536]{1,0:T(8,128)(2,1)S(1)} %copy-done.68, bf16[1536,2048]{1,0:T(8,128)(2,1)} %all-gather.6.cloned.1.call-done), kind=kOutput, calls=%fused_computation.283 | convolution fusion | flops 3222274048 | bytes 14155776 | tf_op jit(solution)/shard_map/dot_general | solution.py:137
  382.9 6.1 %collective-permute-done.59 = bf16[16,3072]{1,0:T(8,128)(2,1)S(1)} collective-permute-done((bf16[16,3072]{1,0:T(8,128)(2,1)S(1)}, bf16[16,3072]{1,0:T(8,128)(2,1)S(1)}, u32[]{:S(2)}, u32[]{:S(2)}) %collective-permute-start.59) | collective-permute-done | bytes 98336 | tf_op jit(solution)/shard_map/ppermute | solution.py:24
  389.2 11.9 %collective-permute-done.60 = bf16[16,3072]{1,0:T(8,128)(2,1)S(1)} collective-permute-done((bf16[16,3072]{1,0:T(8,128)(2,1)S(1)}, bf16[16,3072]{1,0:T(8,128)(2,1)S(1)}, u32[]{:S(2)}, u32[]{:S(2)}) %collective-permute-start.60) | collective-permute-done | bytes 98336 | tf_op jit(solution)/shard_map/ppermute | solution.py:24
  402.0 6.1 %collective-permute-done.61 = bf16[16,3072]{1,0:T(8,128)(2,1)S(1)} collective-permute-done((bf16[16,3072]{1,0:T(8,128)(2,1)S(1)}, bf16[16,3072]{1,0:T(8,128)(2,1)S(1)}, u32[]{:S(2)}, u32[]{:S(2)}) %collective-permute-start.61) | collective-permute-done | bytes 98336 | tf_op jit(solution)/shard_map/ppermute | solution.py:24
  413.1 3.7 fusion.13
  416.8 7.8 %collective-permute-done.63 = bf16[16,18432]{1,0:T(8,128)(2,1)S(1)} collective-permute-done((bf16[16,18432]{1,0:T(8,128)(2,1)S(1)}, bf16[16,18432]{1,0:T(8,128)(2,1)S(1)}, u32[]{:S(2)}, u32[]{:S(2)}) %collective-permute-start.63) | collective-permute-done | bytes 589856 | tf_op jit(solution)/shard_map/ppermute | solution.py:24
  435.9 4.1 collective-permute-done.64
  (481 shorter events, 239.2 us)
Async XLA Ops:
  7.2 44.4 %all-gather.4.cloned.1.call-start = ((), (), s32[]{:S(2)}) async-start(), calls=%async_computation.3 | async-start | bytes 2359296 | tf_op jit(solution)/shard_map/all_gather | solution.py:497
  7.9 104.0 %all-gather.6.cloned.1.call-start = ((), (), s32[]{:S(2)}) async-start(), calls=%async_computation.4 | async-start | bytes 7077888 | tf_op jit(solution)/shard_map/all_gather | solution.py:504
  8.0 23.9 %collective-permute-start.3 = (bf16[128,2048]{1,0:T(8,128)(2,1)}, bf16[128,2048]{1,0:T(8,128)(2,1)}, u32[]{:S(2)}, u32[]{:S(2)}) collective-permute-start(bf16[128,2048]{1,0:T(8,128)(2,1)} %bitcast.211), channel_id=1, source_target_pairs={{0,96},{32,0},{64,32},{96,64},{1,97},{33,1},{65,33},{97,65},{2,98}... | collective-permute-start | bytes 1572872 | tf_op jit(solution)/shard_map/ppermute | solution.py:24
  12.1 19.8 %collective-permute-start.4 = (bf16[128,2048]{1,0:T(8,128)(2,1)}, bf16[128,2048]{1,0:T(8,128)(2,1)S(1)}, u32[]{:S(2)}, u32[]{:S(2)}) collective-permute-start(bf16[128,2048]{1,0:T(8,128)(2,1)} %bitcast.212), channel_id=1, source_target_pairs={{0,32},{32,64},{64,96},{96,0},{1,33},{33,65},{65,97},{97,1},{2,34}... | collective-permute-start | bytes 1572872 | tf_op jit(solution)/shard_map/ppermute | solution.py:24
  31.9 141.9 %all-gather.8.cloned.1.call-start = ((), (), s32[]{:S(2)}) async-start(), calls=%async_computation.5 | async-start | bytes 14155776 | tf_op jit(solution)/shard_map/all_gather | solution.py:524
  55.3 23.6 %collective-permute-start.13 = (bf16[64,3072]{1,0:T(8,128)(2,1)S(1)}, bf16[64,3072]{1,0:T(8,128)(2,1)S(1)}, u32[]{:S(2)}, u32[]{:S(2)}) collective-permute-start(bf16[64,3072]{1,0:T(8,128)(2,1)S(1)} %pad_maximum_fusion.16), channel_id=1, source_target_pairs={{0,32},{32,64},{64,96},{96,0},{1,33},{33,65},{65,97},{97,1},{2,34}... | collective-permute-start | bytes 1179656 | tf_op jit(solution)/shard_map/ppermute | solution.py:24
  55.4 23.5 %collective-permute-start.14 = (bf16[64,3072]{1,0:T(8,128)(2,1)S(1)}, bf16[64,3072]{1,0:T(8,128)(2,1)S(1)}, u32[]{:S(2)}, u32[]{:S(2)}) collective-permute-start(bf16[64,3072]{1,0:T(8,128)(2,1)S(1)} %pad_maximum_fusion.17), channel_id=1, source_target_pairs={{0,64},{32,96},{64,0},{96,32},{1,65},{33,97},{65,1},{97,33},{2,66}... | collective-permute-start | bytes 1179656 | tf_op jit(solution)/shard_map/ppermute | solution.py:24
  62.6 16.2 %collective-permute-start.15 = (bf16[64,3072]{1,0:T(8,128)(2,1)S(1)}, bf16[64,3072]{1,0:T(8,128)(2,1)S(1)}, u32[]{:S(2)}, u32[]{:S(2)}) collective-permute-start(bf16[64,3072]{1,0:T(8,128)(2,1)S(1)} %pad_maximum_fusion.18), channel_id=1, source_target_pairs={{0,96},{32,0},{64,32},{96,64},{1,97},{33,1},{65,33},{97,65},{2,98}... | collective-permute-start | bytes 1179656 | tf_op jit(solution)/shard_map/ppermute | solution.py:24
  82.3 219.8 %reduce-scatter.4.cloned.1.call-start = ((), (), s32[]{:S(2)}) async-start(), calls=%async_computation.6 | async-start | bytes 14155776 | tf_op jit(solution)/shard_map/reduce_scatter | solution.py:495
  82.3 28.8 %collective-permute-start.19 = (bf16[128,2048]{1,0:T(8,128)(2,1)}, bf16[128,2048]{1,0:T(8,128)(2,1)S(1)}, u32[]{:S(2)}, u32[]{:S(2)}) collective-permute-start(bf16[128,2048]{1,0:T(8,128)(2,1)} %bitcast.215), channel_id=1, source_target_pairs={{0,32},{32,64},{64,96},{96,0},{1,33},{33,65},{65,97},{97,1},{2,34}... | collective-permute-start | bytes 1572872 | tf_op jit(solution)/shard_map/ppermute | solution.py:24
  82.4 29.5 %collective-permute-start.18 = (bf16[128,2048]{1,0:T(8,128)(2,1)}, bf16[128,2048]{1,0:T(8,128)(2,1)}, u32[]{:S(2)}, u32[]{:S(2)}) collective-permute-start(bf16[128,2048]{1,0:T(8,128)(2,1)} %bitcast.216), channel_id=1, source_target_pairs={{0,96},{32,0},{64,32},{96,64},{1,97},{33,1},{65,33},{97,65},{2,98}... | collective-permute-start | bytes 1572872 | tf_op jit(solution)/shard_map/ppermute | solution.py:24
  128.1 16.1 %collective-permute-start.21 = (bf16[128,2048]{1,0:T(8,128)(2,1)S(1)}, bf16[128,2048]{1,0:T(8,128)(2,1)S(1)}, u32[]{:S(2)}, u32[]{:S(2)}) collective-permute-start(bf16[128,2048]{1,0:T(8,128)(2,1)S(1)} %pad_maximum_fusion.6), channel_id=1, source_target_pairs={{0,32},{32,64},{64,96},{96,0},{1,33},{33,65},{65,97},{97,1},{2,34}... | collective-permute-start | bytes 1572872 | tf_op jit(solution)/shard_map/ppermute | solution.py:24
  130.4 17.2 %collective-permute-start.25 = (bf16[64,2048]{1,0:T(8,128)(2,1)S(1)}, bf16[64,2048]{1,0:T(8,128)(2,1)S(1)}, u32[]{:S(2)}, u32[]{:S(2)}) collective-permute-start(bf16[64,2048]{1,0:T(8,128)(2,1)S(1)} %slice.293), channel_id=1, source_target_pairs={{0,32},{32,64},{64,96},{96,0},{1,33},{33,65},{65,97},{97,1},{2,34}... | collective-permute-start | bytes 786440 | tf_op jit(solution)/shard_map/ppermute | solution.py:24
  130.5 15.6 %collective-permute-start.24 = (bf16[64,2048]{1,0:T(8,128)(2,1)S(1)}, bf16[64,2048]{1,0:T(8,128)(2,1)S(1)}, u32[]{:S(2)}, u32[]{:S(2)}) collective-permute-start(bf16[64,2048]{1,0:T(8,128)(2,1)S(1)} %slice.292), channel_id=1, source_target_pairs={{0,96},{32,0},{64,32},{96,64},{1,97},{33,1},{65,33},{97,65},{2,98}... | collective-permute-start | bytes 786440 | tf_op jit(solution)/shard_map/ppermute | solution.py:24
  147.7 16.5 %collective-permute-start.28 = (bf16[128,2048]{1,0:T(8,128)(2,1)S(1)}, bf16[128,2048]{1,0:T(8,128)(2,1)S(1)}, u32[]{:S(2)}, u32[]{:S(2)}) collective-permute-start(bf16[128,2048]{1,0:T(8,128)(2,1)S(1)} %get-tuple-element.183), channel_id=1, source_target_pairs={{0,32},{32,64},{64,96},{96,0},{1,33},{33,65},{65,97},{97,1},{2,34}... | collective-permute-start | bytes 1572872 | tf_op jit(solution)/shard_map/ppermute | solution.py:24
  207.8 169.0 %reduce-scatter.6.cloned.1.call-start = ((), (), s32[]{:S(2)}) async-start(), calls=%async_computation.7 | async-start | bytes 2359296 | tf_op jit(solution)/shard_map/reduce_scatter | solution.py:495
  238.1 17.5 %collective-permute-start.36 = (bf16[4,4,48,2048]{3,2,1,0:T(8,128)(2,1)}, bf16[4,4,48,2048]{3,2,1,0:T(8,128)(2,1)}, u32[]{:S(2)}, u32[]{:S(2)}) collective-permute-start(bf16[4,4,48,2048]{3,2,1,0:T(8,128)(2,1)} %dynamic-slice_bitcast_fusion), channel_id=1, source_target_pairs={{0,4},{4,0},{8,12},{12,8},{16,20},{20,16},{24,28},{28,24},{1,5},{5... | collective-permute-start | bytes 9437192 | tf_op jit(solution)/shard_map/ppermute | solution.py:36
  278.5 23.6 %collective-permute-start.42 = (bf16[4,48,2048]{2,1,0:T(8,128)(2,1)}, bf16[4,48,2048]{2,1,0:T(8,128)(2,1)}, u32[]{:S(2)}, u32[]{:S(2)}) collective-permute-start(bf16[4,48,2048]{2,1,0:T(8,128)(2,1)} %pad_maximum_fusion.3), channel_id=1, source_target_pairs={{0,3},{1,0},{2,1},{3,2},{4,7},{5,4},{6,5},{7,6},{8,11},{9,8},{10,9... | collective-permute-start | bytes 2359304 | tf_op jit(solution)/shard_map/ppermute | solution.py:24
  282.5 19.5 %collective-permute-start.41 = (bf16[4,48,2048]{2,1,0:T(8,128)(2,1)}, bf16[4,48,2048]{2,1,0:T(8,128)(2,1)}, u32[]{:S(2)}, u32[]{:S(2)}) collective-permute-start(bf16[4,48,2048]{2,1,0:T(8,128)(2,1)} %pad_maximum_fusion.2), channel_id=1, source_target_pairs={{0,1},{1,2},{2,3},{3,0},{4,5},{5,6},{6,7},{7,4},{8,9},{9,10},{10,1... | collective-permute-start | bytes 2359304 | tf_op jit(solution)/shard_map/ppermute | solution.py:24
  302.1 122.6 %reduce-scatter.8.cloned.1.call-start = ((), (), s32[]{:S(2)}) async-start(), calls=%async_computation.8 | async-start | bytes 4128768 | tf_op jit(solution)/shard_map/reduce_scatter | solution.py:495
  344.3 22.4 %collective-permute-start.48 = (bf16[64,2048]{1,0:T(8,128)(2,1)}, bf16[64,2048]{1,0:T(8,128)(2,1)S(1)}, u32[]{:S(2)}, u32[]{:S(2)}) collective-permute-start(bf16[64,2048]{1,0:T(8,128)(2,1)} %get-tuple-element.205), channel_id=1, source_target_pairs={{0,32},{32,64},{64,96},{96,0},{1,33},{33,65},{65,97},{97,1},{2,34}... | collective-permute-start | bytes 786440 | tf_op jit(solution)/shard_map/ppermute | solution.py:24
  344.3 22.4 %collective-permute-start.50 = (bf16[64,2048]{1,0:T(8,128)(2,1)}, bf16[64,2048]{1,0:T(8,128)(2,1)S(1)}, u32[]{:S(2)}, u32[]{:S(2)}) collective-permute-start(bf16[64,2048]{1,0:T(8,128)(2,1)} %get-tuple-element.206), channel_id=1, source_target_pairs={{0,96},{32,0},{64,32},{96,64},{1,97},{33,1},{65,33},{97,65},{2,98}... | collective-permute-start | bytes 786440 | tf_op jit(solution)/shard_map/ppermute | solution.py:24
  348.9 22.9 %collective-permute-start.54 = (bf16[4,16,3072]{2,1,0:T(8,128)(2,1)S(1)}, bf16[4,16,3072]{2,1,0:T(8,128)(2,1)S(1)}, u32[]{:S(2)}, u32[]{:S(2)}) collective-permute-start(bf16[4,16,3072]{2,1,0:T(8,128)(2,1)S(1)} %get-tuple-element.217), channel_id=1, source_target_pairs={{0,1},{1,2},{2,3},{3,0},{4,5},{5,6},{6,7},{7,4},{8,9},{9,10},{10,1... | collective-permute-start | bytes 1179656 | tf_op jit(solution)/shard_map/ppermute | solution.py:24
  349.3 23.8 %collective-permute-start.56 = (bf16[4,16,3072]{2,1,0:T(8,128)(2,1)S(1)}, bf16[4,16,3072]{2,1,0:T(8,128)(2,1)S(1)}, u32[]{:S(2)}, u32[]{:S(2)}) collective-permute-start(bf16[4,16,3072]{2,1,0:T(8,128)(2,1)S(1)} %get-tuple-element.218), channel_id=1, source_target_pairs={{0,3},{1,0},{2,1},{3,2},{4,7},{5,4},{6,5},{7,6},{8,11},{9,8},{10,9... | collective-permute-start | bytes 1179656 | tf_op jit(solution)/shard_map/ppermute | solution.py:24
  352.6 21.5 %collective-permute-start.55 = (bf16[4,16,3072]{2,1,0:T(8,128)(2,1)S(1)}, bf16[4,16,3072]{2,1,0:T(8,128)(2,1)S(1)}, u32[]{:S(2)}, u32[]{:S(2)}) collective-permute-start(bf16[4,16,3072]{2,1,0:T(8,128)(2,1)S(1)} %get-tuple-element.219), channel_id=1, source_target_pairs={{0,2},{1,3},{2,0},{3,1},{4,6},{5,7},{6,4},{7,5},{8,10},{9,11},{10,... | collective-permute-start | bytes 1179656 | tf_op jit(solution)/shard_map/ppermute | solution.py:24
  371.8 41.3 %collective-permute-start.51 = (bf16[128,2048]{1,0:T(8,128)(2,1)}, bf16[128,2048]{1,0:T(8,128)(2,1)}, u32[]{:S(2)}, u32[]{:S(2)}) collective-permute-start(bf16[128,2048]{1,0:T(8,128)(2,1)} %pad_maximum_fusion.11), channel_id=1, source_target_pairs={{0,96},{32,0},{64,32},{96,64},{1,97},{33,1},{65,33},{97,65},{2,98}... | collective-permute-start | bytes 1572872 | tf_op jit(solution)/shard_map/ppermute | solution.py:24
  373.1 40.0 %collective-permute-start.49 = (bf16[128,2048]{1,0:T(8,128)(2,1)}, bf16[128,2048]{1,0:T(8,128)(2,1)}, u32[]{:S(2)}, u32[]{:S(2)}) collective-permute-start(bf16[128,2048]{1,0:T(8,128)(2,1)} %pad_maximum_fusion.10), channel_id=1, source_target_pairs={{0,32},{32,64},{64,96},{96,0},{1,33},{33,65},{65,97},{97,1},{2,34}... | collective-permute-start | bytes 1572872 | tf_op jit(solution)/shard_map/ppermute | solution.py:24
  379.3 28.9 %collective-permute-start.57 = (bf16[128,2048]{1,0:T(8,128)(2,1)S(1)}, bf16[128,2048]{1,0:T(8,128)(2,1)S(1)}, u32[]{:S(2)}, u32[]{:S(2)}) collective-permute-start(bf16[128,2048]{1,0:T(8,128)(2,1)S(1)} %pad_maximum_fusion.12), channel_id=1, source_target_pairs={{0,32},{32,64},{64,96},{96,0},{1,33},{33,65},{65,97},{97,1},{2,34}... | collective-permute-start | bytes 1572872 | tf_op jit(solution)/shard_map/ppermute | solution.py:24
  382.8 25.4 %collective-permute-start.58 = (bf16[128,2048]{1,0:T(8,128)(2,1)S(1)}, bf16[128,2048]{1,0:T(8,128)(2,1)S(1)}, u32[]{:S(2)}, u32[]{:S(2)}) collective-permute-start(bf16[128,2048]{1,0:T(8,128)(2,1)S(1)} %pad_maximum_fusion.13), channel_id=1, source_target_pairs={{0,96},{32,0},{64,32},{96,64},{1,97},{33,1},{65,33},{97,65},{2,98}... | collective-permute-start | bytes 1572872 | tf_op jit(solution)/shard_map/ppermute | solution.py:24
  408.4 16.1 %collective-permute-start.63 = (bf16[16,18432]{1,0:T(8,128)(2,1)S(1)}, bf16[16,18432]{1,0:T(8,128)(2,1)S(1)}, u32[]{:S(2)}, u32[]{:S(2)}) collective-permute-start(bf16[16,18432]{1,0:T(8,128)(2,1)S(1)} %constant_dynamic-update-slice_fusion.36), channel_id=1, source_target_pairs={{0,1},{1,2},{2,3},{3,0},{4,5},{5,6},{6,7},{7,4},{8,9},{9,10},{10,1... | collective-permute-start | bytes 1769480 | tf_op jit(solution)/shard_map/ppermute | solution.py:24
  425.7 17.6 %collective-permute-start.68 = (bf16[8,18432]{1,0:T(8,128)(2,1)S(1)}, bf16[8,18432]{1,0:T(8,128)(2,1)S(1)}, u32[]{:S(2)}, u32[]{:S(2)}) collective-permute-start(bf16[8,18432]{1,0:T(8,128)(2,1)S(1)} %slice.342), channel_id=1, source_target_pairs={{0,1},{1,2},{2,3},{3,0},{4,5},{5,6},{6,7},{7,4},{8,9},{9,10},{10,1... | collective-permute-start | bytes 884744 | tf_op jit(solution)/shard_map/ppermute | solution.py:24
  426.4 16.9 %collective-permute-start.67 = (bf16[8,18432]{1,0:T(8,128)(2,1)S(1)}, bf16[8,18432]{1,0:T(8,128)(2,1)S(1)}, u32[]{:S(2)}, u32[]{:S(2)}) collective-permute-start(bf16[8,18432]{1,0:T(8,128)(2,1)S(1)} %slice.341), channel_id=1, source_target_pairs={{0,3},{1,0},{2,1},{3,2},{4,7},{5,4},{6,5},{7,6},{8,11},{9,8},{10,9... | collective-permute-start | bytes 884744 | tf_op jit(solution)/shard_map/ppermute | solution.py:24
  (120 other events, 1002.6 us)
Sparse Core Ops, SparseCore 0:
  9.7 26.6 all-gather.3
  38.1 44.9 all-gather.5
  85.3 67.6 all-gather.7
  208.0 70.9 reduce-scatter.3
  302.2 38.6 reduce-scatter.5
  376.9 31.3 reduce-scatter.7

commit v2 on v1

--- a/solution.py
+++ b/solution.py
@@ -58,7 +58,8 @@
 
 
 def scatter_ring(parts, axis):
-    own, nxt, far, prv = parts
+    far = parts[2]
+    own, nxt, prv = [parts[i].astype(jnp.float32) for i in (0, 1, 3)]
     half = own.shape[0] // 2
     got_a = send(far[:half].astype(jnp.bfloat16), axis, 1).astype(jnp.float32)
     got_b = send(far[half:].astype(jnp.bfloat16), axis, -1).astype(jnp.float32)
@@ -86,8 +87,13 @@
 
 
 def ordered(parts, index):
-    twice = jnp.stack(parts + parts, axis=0)
-    return lax.dynamic_slice_in_dim(twice, (RING - index) % RING, RING, 0)
+    return jnp.stack(
+        [
+            lax.select_n(index, *[parts[(place - m) % RING] for m in range(RING)])
+            for place in range(RING)
+        ],
+        axis=0,
+    )
 
 
 def exchange_parts(pick, axis, index):
@@ -294,19 +300,20 @@
 
 def project_kernel(
     info, tok_ref, cos_ref, sin_ref, own, after, far_a, far_b, before, near, far,
-    n_ref, q_ref, kv_ref, gains_ref, w_ref, sems, *, heads, block
+    n_ref, q_ref, kv_ref, scale_ref, gains_ref, w_ref, sems, *, heads, block
 ):
     q_cols = heads * HD
 
     @pl.when(pl.program_id(0) == 0)
     def _():
-        x, core = info[0] // 2, info[0] % 2
+        x, core, seq = info[0] // 2, info[0] % 2, info[1]
         copies = []
 
         def fetch(piece, k, other, first):
             place = (x + k) % RING * 2 + (1 - core if other else core)
             for i in range(piece.shape[0]):
-                at = pl.multiple_of((first + i) * 8 * block + place * block, block)
+                source = (seq - first - i + RING) % RING
+                at = pl.multiple_of(source * 8 * block + place * block, block)
                 copies.append(
                     pltpu.make_async_copy(
                         piece.at[i], w_ref.at[pl.ds(at, block), :], sems.at[len(copies)]
@@ -336,6 +343,7 @@
     scale = lax.rsqrt(jnp.mean(x * x, axis=1, keepdims=True) + epsilon)
     normed = (x * scale * gains_ref[0:1, :]).astype(jnp.bfloat16)
     n_ref[...] = normed
+    scale_ref[...] = jnp.broadcast_to(scale, scale_ref.shape)
     qkv = jnp.dot(normed, w_ref[:, : q_cols + 2 * HD], preferred_element_type=jnp.float32)
     cos, sin = cos_ref[...], sin_ref[...]
     for h in range(heads + 1):
@@ -363,6 +371,7 @@
             rows(width),
             rows(heads * HD),
             rows(2 * HD),
+            rows(HD),
             whole((8, width)),
             whole((width, columns)),
         ],
@@ -370,6 +379,7 @@
             jax.ShapeDtypeStruct((group, width), jnp.bfloat16),
             jax.ShapeDtypeStruct((group, heads * HD), jnp.bfloat16),
             jax.ShapeDtypeStruct((group, 2 * HD), jnp.bfloat16),
+            jax.ShapeDtypeStruct((group, HD), jnp.float32),
             jax.ShapeDtypeStruct((8, width), jnp.float32),
             jax.ShapeDtypeStruct((width, columns), jnp.bfloat16),
         ],
@@ -379,7 +389,59 @@
     )(info, tokens, cos, sin, *pieces)
 
 
-def feed_kernel(n_ref, gh_ref, gate_ref, up_ref, hidden_ref, grad_ref, back_ref):
+def unproject_kernel(
+    dq_ref, dkv_ref, w_ref, n_ref, tok_ref, scale_ref, att_ref, branch_ref, two_ref,
+    part_ref, grad_ref
+):
+    q_cols = dq_ref.shape[1]
+    n_attn = w_ref.shape[1]
+    grads = jnp.concatenate([dq_ref[...], dkv_ref[...]], axis=1)
+    part = inner_cols(grads, w_ref[:, : q_cols + 2 * HD])
+    part_ref[...] = part.astype(jnp.bfloat16)
+    terms = (part * tok_ref[...].astype(jnp.float32) * scale_ref[:, 0:1]).astype(jnp.bfloat16)
+    column = lax.broadcasted_iota(jnp.int32, (part.shape[0], HD), 1)
+    first = (column == 0).astype(jnp.bfloat16)
+    second = (column == 1).astype(jnp.bfloat16)[: two_ref.shape[0]]
+    grad_ref[:, : q_cols + 2 * HD] = inner_rows(n_ref[...], grads).astype(jnp.bfloat16)
+    gains = inner_rows(terms, first) + inner_rows(two_ref[...], second)
+    grad_ref[:, q_cols + 2 * HD : n_attn] = gains.astype(jnp.bfloat16)
+    grad_ref[:, n_attn:] = inner_rows(att_ref[...], branch_ref[...]).astype(jnp.bfloat16)
+
+
+def unproject(
+    grad_queries, grad_pair, weights, normed, tokens, scale, attended, grad_branch, two
+):
+    group, width = tokens.shape
+    size = 4 * BLOCK
+    columns = weights.shape[1]
+    whole = lambda n: pl.BlockSpec((group, n), lambda i: (0, 0))
+    across = pl.BlockSpec((group, size), lambda i: (0, i))
+    down = pl.BlockSpec((size, columns), lambda i: (i, 0))
+    return pl.pallas_call(
+        unproject_kernel,
+        grid=(width // size,),
+        in_specs=[
+            whole(grad_queries.shape[1]),
+            whole(grad_pair.shape[1]),
+            down,
+            across,
+            across,
+            whole(HD),
+            whole(attended.shape[1]),
+            across,
+            pl.BlockSpec((two.shape[0], size), lambda i: (0, i)),
+        ],
+        out_specs=[across, pl.BlockSpec((size, columns + size), lambda i: (i, 0))],
+        out_shape=[
+            jax.ShapeDtypeStruct((group, width), jnp.bfloat16),
+            jax.ShapeDtypeStruct((width, columns + size), jnp.bfloat16),
+        ],
+        compiler_params=pltpu.CompilerParams(vmem_limit_bytes=40 * 1024 * 1024),
+        name="unproject",
+    )(grad_queries, grad_pair, weights, normed, tokens, scale, attended, grad_branch, two)
+
+
+def feed_kernel(n_ref, gh_ref, gate_ref, up_ref, hidden_ref, grad_ref):
     step = pl.program_id(0)
     size = gate_ref.shape[1]
     inner = grad_ref.shape[1] // 2
@@ -397,15 +459,6 @@
     grad_upper = (grad_hidden * act).astype(jnp.bfloat16)
     grad_ref[:, pl.ds(pl.multiple_of(step * size, size), size)] = grad_gate
     grad_ref[:, pl.ds(pl.multiple_of(inner + step * size, size), size)] = grad_upper
-    back = inner_cols(grad_gate, gate_ref[...]) + inner_cols(grad_upper, up_ref[...])
-
-    @pl.when(step == 0)
-    def _():
-        back_ref[...] = back
-
-    @pl.when(step > 0)
-    def _():
-        back_ref[...] += back
 
 
 def feed(normed, grad_hidden, weights):
@@ -423,20 +476,82 @@
             pl.BlockSpec((width, FBLOCK), lambda i: (0, i)),
             pl.BlockSpec((width, FBLOCK), lambda i: (0, steps + i)),
         ],
-        out_specs=[columns, whole(2 * inner), whole(width)],
+        out_specs=[columns, whole(2 * inner)],
         out_shape=[
             jax.ShapeDtypeStruct((group, inner), jnp.bfloat16),
             jax.ShapeDtypeStruct((group, 2 * inner), jnp.bfloat16),
-            jax.ShapeDtypeStruct((group, width), jnp.float32),
-        ],
-        compiler_params=pltpu.CompilerParams(vmem_limit_bytes=56 * 1024 * 1024),
-        cost_estimate=pl.CostEstimate(
-            flops=8 * group * width * inner,
-            bytes_accessed=4 * width * inner,
-            transcendentals=group * inner,
-        ),
+        ],
+        compiler_params=pltpu.CompilerParams(vmem_limit_bytes=48 * 1024 * 1024),
         name="feed",
     )(normed, grad_hidden, weights, weights)
+
+
+def back_kernel(left_ref, right_ref, out_ref):
+    out_ref[...] = inner_cols(left_ref[...], right_ref[...]).astype(jnp.bfloat16)
+
+
+def back(left, right):
+    rows, inner = left.shape
+    columns = right.shape[0]
+    size = 2 * BLOCK
+    return pl.pallas_call(
+        back_kernel,
+        grid=(columns // size,),
+        in_specs=[
+            pl.BlockSpec((rows, inner), lambda i: (0, 0)),
+            pl.BlockSpec((size, inner), lambda i: (i, 0)),
+        ],
+        out_specs=pl.BlockSpec((rows, size), lambda i: (0, i)),
+        out_shape=jax.ShapeDtypeStruct((rows, columns), jnp.bfloat16),
+        compiler_params=pltpu.CompilerParams(vmem_limit_bytes=40 * 1024 * 1024),
+        name="back",
+    )(left, right)
+
+
+def outer_kernel(left_ref, right_ref, out_ref):
+    out_ref[...] = inner_rows(left_ref[...], right_ref[...]).astype(jnp.bfloat16)
+
+
+def outer(left, right):
+    rows, wide = left.shape
+    columns = right.shape[1]
+    size = 2 * BLOCK
+    return pl.pallas_call(
+        outer_kernel,
+        grid=(wide // size,),
+        in_specs=[
+            pl.BlockSpec((rows, size), lambda i: (0, i)),
+            pl.BlockSpec((rows, columns), lambda i: (0, 0)),
+        ],
+        out_specs=pl.BlockSpec((size, columns), lambda i: (i, 0)),
+        out_shape=jax.ShapeDtypeStruct((wide, columns), jnp.bfloat16),
+        compiler_params=pltpu.CompilerParams(vmem_limit_bytes=40 * 1024 * 1024),
+        name="outer",
+    )(left, right)
+
+
+def times_kernel(left_ref, right_ref, out_ref):
+    out_ref[...] = jnp.dot(
+        left_ref[...], right_ref[...], preferred_element_type=jnp.float32
+    ).astype(jnp.bfloat16)
+
+
+def times(left, right):
+    rows, inner = left.shape
+    columns = right.shape[1]
+    size = 4 * BLOCK
+    return pl.pallas_call(
+        times_kernel,
+        grid=(columns // size,),
+        in_specs=[
+            pl.BlockSpec((rows, inner), lambda i: (0, 0)),
+            pl.BlockSpec((inner, size), lambda i: (0, i)),
+        ],
+        out_specs=pl.BlockSpec((rows, size), lambda i: (0, i)),
+        out_shape=jax.ShapeDtypeStruct((rows, columns), jnp.bfloat16),
+        compiler_params=pltpu.CompilerParams(vmem_limit_bytes=40 * 1024 * 1024),
+        name="times",
+    )(left, right)
 
 
 def shards(
@@ -502,7 +617,7 @@
         *got, tok_after, tok_before, gate_weight, up_weight, down_weight
     )
     w_down = lax.all_gather(down_weight, "shard", axis=0, tiled=True)
-    block = by_source(got, seq_index)
+    block = jnp.stack(got)
     block_after = send_x(block, -1)
     block_before = send_x(block, 1)
     half = rows // 2
@@ -515,19 +630,21 @@
     block_far_b = send_x(block_before[RING // 2 :], 1)
     near = send_core(jnp.stack([block, block_after, block_before]))
     got = exchange_parts(pick_f, "seq", seq_index)
-    block_far_a, block_far_b, near = fence(block_far_a, block_far_b, near)
+    tokens_bf = jnp.concatenate([own_tokens, tok_after, tok_far_a, tok_far_b, tok_before], axis=0)
+    block_far_a, block_far_b, near, tokens_bf = fence(block_far_a, block_far_b, near, tokens_bf)
     far = send_core(jnp.concatenate([block_far_a, block_far_b]))
-    tokens_bf = jnp.concatenate([own_tokens, tok_after, tok_far_a, tok_far_b, tok_before], axis=0)
     pieces = (block, block_after, block_far_a, block_far_b, block_before, near, far)
-    normed_one, queries, pair, gain_rows, w_attn = project(info, tokens_bf, cos, sin, pieces)
+    normed_one, queries, pair, scale_one, gain_rows, w_attn = project(
+        info, tokens_bf, cos, sin, pieces
+    )
     *got, own_cotangent, pair = fence(*got, own_cotangent, pair)
     w_ff = lax.all_gather(by_source(got, seq_index), "shard", axis=1, tiled=True)
     w_ff = w_ff.reshape(width, -1)
-    gain_one, gain_two = gain_rows[0], gain_rows[1]
-    w_qkv = w_attn[:, : q_cols + 2 * HD]
+    kvs = [shifted(pair, "shard", 2), shifted(pair, "shard", 1), pair]
+    *kvs, own_cotangent = fence(*kvs, own_cotangent)
     cot_after = send(own_cotangent, "seq", -1)
     cot_before = send(own_cotangent, "seq", 1)
-    kvs = [shifted(pair, "shard", 2), shifted(pair, "shard", 1), pair]
+    gain_one, gain_two = gain_rows[0], gain_rows[1]
     attended, lse = attend(info, queries, kvs)
     attended, cot_after, cot_before, w_down = fence(attended, cot_after, cot_before, w_down)
     cot_far_a = send(cot_after[:half], "seq", -1)
@@ -542,151 +659,137 @@
     normed_two = (middle * scale_two * gain_two).astype(jnp.bfloat16)
     normed_two = jnp.concatenate(gather_ring(normed_two, "seq"), axis=0)
     grad_hidden, normed_two = fence(inner_cols(all_cotangent, w_down), normed_two)
-    hidden, grad_ff, partial_two = feed(normed_two, grad_hidden, w_ff)
-    grad_wff = inner_rows(normed_two, grad_ff).astype(jnp.bfloat16)
-    grad_down = inner_rows(hidden, all_cotangent).astype(jnp.bfloat16)
+    hidden, grad_ff = feed(normed_two, grad_hidden, w_ff)
+    grad_down = outer(hidden, all_cotangent)
+    share_down = scattered(grad_down, 0)
+    grad_down, grad_ff = fence(grad_down, grad_ff)
+    partial_two = back(grad_ff, w_ff)
+    part = own_rows // RING
+
+    def first_half(parts):
+        return send(parts[2][:half], "seq", 1), send(parts[2][half:], "seq", -1)
+
+    def second_half(parts, got_a, got_b):
+        one, last = [parts[i].astype(jnp.float32) for i in (1, 3)]
+        one = jnp.concatenate([one[:half] + got_a.astype(jnp.float32), one[half:]], axis=0)
+        last = jnp.concatenate([last[:half], last[half:] + got_b.astype(jnp.float32)], axis=0)
+        return (
+            send(one.astype(jnp.bfloat16), "seq", 1),
+            send(last.astype(jnp.bfloat16), "seq", -1),
+        )
+
+    def total(*blocks):
+        return sum(block.astype(jnp.float32) for block in blocks)
+
+    parts = row_blocks(partial_two)
+    two_a, two_b = first_half(parts)
+    two_a, two_b, grad_ff = fence(two_a, two_b, grad_ff)
+    from_last, from_next = second_half(parts, two_a, two_b)
+    grad_wff = outer(normed_two, grad_ff)
+    from_last, from_next, grad_wff, hidden = fence(from_last, from_next, grad_wff, hidden)
     share_ff = scattered(grad_wff.reshape(RING, -1, 2 * f_cols), 1)
-    grad_normed_two = scatter_ring(row_blocks(partial_two), "seq")
-    grad_normed_two, grad_wff, grad_down = fence(grad_normed_two, grad_wff, grad_down)
-
-    x_index, core = shard_index // 2, shard_index % 2
-    part = own_rows // RING
-    grad_down = grad_down.reshape(RING, 2, RING, -1, width)
-    down_other = send_core(lax.dynamic_index_in_dim(grad_down, 1 - core, 1, keepdims=False))
+    grad_normed_two = total(parts[0], from_last, from_next)
     grad_middle = own_cotangent.astype(jnp.float32) + norm_back(
         middle, scale_two, gain_two, grad_normed_two
     )
-    gain_two_terms = (grad_normed_two * middle * scale_two).astype(jnp.bfloat16)
     own_branch = grad_middle.astype(jnp.bfloat16)
+
     gb_after = send(own_branch, "seq", -1)
     gb_before = send(own_branch, "seq", 1)
-    gb_after, gb_before, down_other, grad_down = fence(gb_after, gb_before, down_other, grad_down)
+    out_parts = times(hidden, w_down)
+    gb_after, gb_before, out_parts = fence(gb_after, gb_before, out_parts)
+    out_parts = row_blocks(out_parts)
     gb_far_a = send(gb_after[:half], "seq", -1)
     gb_far_b = send(gb_before[half:], "seq", 1)
-    mine = lax.dynamic_index_in_dim(grad_down, core, 1, keepdims=False).astype(jnp.float32)
-    mine = (mine + down_other.astype(jnp.float32)).astype(jnp.bfloat16)
-    down_parts = [
-        lax.dynamic_index_in_dim(mine, (grp_index + k) % RING, 1, keepdims=False)
-        for k in range(RING)
-    ]
-    down_a = send(down_parts[2][: RING // 2], "grp", 1)
-    down_b = send(down_parts[2][RING // 2 :], "grp", -1)
-    gb_far_a, gb_far_b, down_a, down_b, *down_parts = fence(
-        gb_far_a, gb_far_b, down_a, down_b, *down_parts
-    )
+    gb_far_a, gb_far_b, *out_parts = fence(gb_far_a, gb_far_b, *out_parts)
     grad_branch = jnp.concatenate([own_branch, gb_after, gb_far_a, gb_far_b, gb_before], axis=0)
     grad_attended = inner_cols(grad_branch, w_out).astype(jnp.bfloat16)
-    down_own, down_next, _, down_last = [one.astype(jnp.float32) for one in down_parts]
-    down_next = jnp.concatenate(
-        [down_next[: RING // 2] + down_a.astype(jnp.float32), down_next[RING // 2 :]], axis=0
-    ).astype(jnp.bfloat16)
-    down_last = jnp.concatenate(
-        [down_last[: RING // 2], down_last[RING // 2 :] + down_b.astype(jnp.float32)], axis=0
-    ).astype(jnp.bfloat16)
-    down_next = send(down_next, "grp", 1)
-    down_last = send(down_last, "grp", -1)
-
+
+    out_a, out_b = first_half(out_parts)
     grad_queries, grad_table = attend_back(info, queries, grad_attended, lse, cos, sin, kvs)
-    grad_wout = inner_rows(attended, grad_branch).astype(jnp.bfloat16)
-    grad_queries, grad_table, share_ff, down_next, down_last, grad_wout = fence(
-        grad_queries, grad_table, share_ff, down_next, down_last, grad_wout
-    )
-    share_out = scattered(grad_wout, 0)
+    grad_queries, grad_table, out_a, out_b, share_down = fence(
+        grad_queries, grad_table, out_a, out_b, share_down
+    )
+
     returned_two = shifted(grad_table[0].astype(jnp.bfloat16), "shard", -2)
     returned_one = shifted(grad_table[1].astype(jnp.bfloat16), "shard", -1)
-    down_own = down_own + down_next.astype(jnp.float32) + down_last.astype(jnp.float32)
-    down_own = scatter_x(
-        lambda i: lax.dynamic_index_in_dim(down_own, i, 0, keepdims=False), x_index
-    ).astype(jnp.bfloat16)
-    returned_one, returned_two, down_own, share_ff, hidden = fence(
-        returned_one, returned_two, down_own, share_ff, hidden
-    )
-    grad_pair = (
-        grad_table[2] + returned_one.astype(jnp.float32) + returned_two.astype(jnp.float32)
-    )
+
+    def grp_pieces(share, dim):
+        return exchange_parts(
+            lambda i: lax.dynamic_index_in_dim(share, i, dim, keepdims=False), "grp", grp_index
+        )
+
+    def seq_pieces(summed):
+        return exchange_parts(
+            lambda i: lax.dynamic_index_in_dim(summed, i, 0, keepdims=False), "seq", seq_index
+        )
+
+    def side_by_side(columns):
+        return columns.transpose(1, 0, 2).reshape(columns.shape[1], -1)
+
+    down_pieces = grp_pieces(share_down.reshape(RING, -1, width), 0)
+    returned_one, returned_two, grad_table, out_a, out_b, *down_pieces = fence(
+        returned_one, returned_two, grad_table, out_a, out_b, *down_pieces
+    )
+    grad_pair = total(grad_table[2], returned_one, returned_two)
     grad_keys = grad_pair[:, :HD]
     swapped = jnp.concatenate([grad_keys[:, HD // 2 :], grad_keys[:, : HD // 2]], axis=1)
     grad_keys = grad_keys * cos - swapped * sin
     grad_pair = jnp.concatenate([grad_keys, grad_pair[:, HD:]], axis=1).astype(jnp.bfloat16)
-    grad_qkv = jnp.concatenate([grad_queries, grad_pair], axis=1)
-    all_tokens = tokens_bf.astype(jnp.float32)
-    scale_one = norm_scale(all_tokens)
-    partial_one = inner_cols(grad_qkv, w_qkv)
-    gain_one_terms = (partial_one * all_tokens * scale_one).astype(jnp.bfloat16)
-    columns = jnp.arange(HD)[None, :]
-    first_column = jnp.broadcast_to(columns == 0, (group_rows, HD)).astype(jnp.bfloat16)
-    second_column = jnp.broadcast_to(columns == 1, (rows, HD)).astype(jnp.bfloat16)
-    grad_gains = inner_rows(gain_one_terms, first_column) + inner_rows(
-        gain_two_terms, second_column
-    )
-    grad_attn = jnp.concatenate(
-        fence(inner_rows(normed_one, grad_qkv).astype(jnp.bfloat16), grad_gains.astype(jnp.bfloat16)),
-        axis=1,
-    )
-
-    def spread(share):
-        share = share.reshape(RING, RING, part, -1)
-        summed = scatter_direct(
-            lambda i: lax.dynamic_index_in_dim(share, i, 1, keepdims=False).astype(jnp.float32),
-            "grp",
-            grp_index,
-        )
-        return summed.astype(jnp.bfloat16)
-
-    def placed(summed):
-        return exchange(
-            lambda i: lax.dynamic_index_in_dim(summed, i, 0, keepdims=False), "seq", seq_index
-        )
-
-    def side_by_side(columns):
-        return columns.transpose(1, 0, 2).reshape(columns.shape[1], -1)
-
-    own_one, next_one, far_one, last_one = row_blocks(partial_one)
-    one_a = send(far_one[:half].astype(jnp.bfloat16), "seq", 1)
-    one_b = send(far_one[half:].astype(jnp.bfloat16), "seq", -1)
-    sum_ff = spread(share_ff)
-    one_a, one_b, sum_ff, grad_attn, share_out = fence(one_a, one_b, sum_ff, grad_attn, share_out)
+    gain_two_terms = (grad_normed_two * middle * scale_two).astype(jnp.bfloat16)
+    partial_one, grad_attn = unproject(
+        grad_queries, grad_pair, w_attn, normed_one, tokens_bf, scale_one, attended, grad_branch,
+        gain_two_terms,
+    )
+    parts = row_blocks(partial_one)
+    one_a, one_b = first_half(parts)
+    n_attn = w_attn.shape[1]
     share_attn = scattered(grad_attn.reshape(RING, -1, grad_attn.shape[1]), 1)
-    next_one = jnp.concatenate([next_one[:half] + one_a.astype(jnp.float32), next_one[half:]], axis=0)
-    last_one = jnp.concatenate([last_one[:half], last_one[half:] + one_b.astype(jnp.float32)], axis=0)
-    from_last = send(next_one.astype(jnp.bfloat16), "seq", 1)
-    from_next = send(last_one.astype(jnp.bfloat16), "seq", -1)
-    ff_columns = placed(sum_ff)
-    from_last, from_next, ff_columns = fence(from_last, from_next, ff_columns)
-    grad_normed_one = own_one + from_last.astype(jnp.float32) + from_next.astype(jnp.float32)
+    down_own = total(*down_pieces).astype(jnp.bfloat16)
+    down_got = [send(down_own, "grp", -k) for k in range(1, RING)]
+    one_a, one_b, out_a, out_b, share_ff, *down_got = fence(
+        one_a, one_b, out_a, out_b, share_ff, *down_got
+    )
+    from_last, from_next = second_half(parts, one_a, one_b)
+    ff_pieces = grp_pieces(share_ff.reshape(RING, RING, part, -1), 1)
+    from_last, from_next, out_a, out_b, *ff_pieces = fence(
+        from_last, from_next, out_a, out_b, *ff_pieces
+    )
+    ff_pieces = seq_pieces(total(*ff_pieces).astype(jnp.bfloat16))
+    out_last, out_next = second_half(out_parts, out_a, out_b)
+    out_last, out_next, *ff_pieces = fence(out_last, out_next, *ff_pieces)
+    result = middle + total(out_parts[0], out_last, out_next)
+    layer_output = result.astype(jnp.bfloat16)[None, None]
+    share_down = ordered([down_own] + down_got, grp_index).reshape(-1, width)
+    share_down = share_down.astype(jnp.float32)
+    ff_columns = by_source(ff_pieces, seq_index)
+    ff_rows = jnp.concatenate(
+        [side_by_side(ff_columns[:, :, :f_cols]), side_by_side(ff_columns[:, :, f_cols:])], axis=1
+    )
+    ff_after = send(ff_rows, "grp", -1)
+    ff_before = send(ff_rows, "grp", 1)
+    grad_normed_one = total(parts[0], from_last, from_next)
     own_inputs = own_tokens.astype(jnp.float32)
     input_grad = grad_middle + norm_back(
         own_inputs, norm_scale(own_inputs), gain_one, grad_normed_one
     )
-    ff_rows = jnp.concatenate(
-        [
-            side_by_side(ff_columns[:, :, :f_cols]),
-            side_by_side(ff_columns[:, :, f_cols:]),
-            down_own.reshape(part, -1),
-        ],
-        axis=1,
-    )
-    ff_after = send(ff_rows, "grp", -1)
-    ff_before = send(ff_rows, "grp", 1)
-    ff_after, ff_before, share_attn, input_grad = fence(ff_after, ff_before, share_attn, input_grad)
+    ff_after, ff_before, input_grad = fence(ff_after, ff_before, input_grad)
     ff_far_a = send(ff_after[: part // 2], "grp", -1)
     ff_far_b = send(ff_before[part // 2 :], "grp", 1)
-
-    from_out = share_out.reshape(RING, part, RING, -1).transpose(2, 0, 1, 3)
-    from_out = from_out.reshape(RING, own_rows, -1)
-    summed = spread(jnp.concatenate([share_attn, from_out], axis=2))
+    ff_far_a, ff_far_b, share_attn = fence(ff_far_a, ff_far_b, share_attn)
+    pieces = grp_pieces(share_attn.reshape(RING, RING, part, -1), 1)
     ff_far = jnp.concatenate([ff_far_a, ff_far_b], axis=0)
-    summed, ff_far = fence(summed, ff_far)
     ff_rows = ordered([ff_rows, ff_after, ff_far, ff_before], grp_index)
     ff_rows = ff_rows.reshape(own_rows, -1).astype(jnp.float32)
     share_gate = ff_rows[:, : RING * f_cols]
-    share_upper = ff_rows[:, RING * f_cols : 2 * RING * f_cols]
-    share_down = ff_rows[:, 2 * RING * f_cols :].reshape(-1, width)
-    n_attn = share_attn.shape[2]
+    share_upper = ff_rows[:, RING * f_cols :]
+    summed = total(*pieces).astype(jnp.bfloat16)
     out_own = side_by_side(summed[:, :, n_attn:])
-    columns = placed(summed[:, :, :n_attn])
-    summed = jnp.sum(columns[:, :, q_cols:].astype(jnp.float32), axis=0).astype(jnp.bfloat16)
-    attn_rows = jnp.concatenate([side_by_side(columns[:, :, :q_cols]), out_own, summed], axis=1)
+    columns = by_source(seq_pieces(summed[:, :, :n_attn]), seq_index)
+    summed = total(*[columns[i, :, q_cols:] for i in range(RING)]).astype(jnp.bfloat16)
+    attn_rows = jnp.concatenate(
+        [side_by_side(columns[:, :, :q_cols]), out_own, summed], axis=1
+    )
     attn_rows = gather_direct(attn_rows, "grp", grp_index).reshape(own_rows, -1)
     attn_rows = attn_rows.astype(jnp.float32)
     share_query = attn_rows[:, :width]
@@ -694,9 +797,6 @@
     share_pair = attn_rows[:, 2 * width : 2 * width + 2 * HD]
     share_gain_one = attn_rows[:, 2 * width + 2 * HD]
     share_gain_two = attn_rows[:, 2 * width + 2 * HD + 1]
-
-    result = middle + scatter_ring(row_blocks(matmul(hidden, w_down)), "seq")
-    layer_output = result.astype(jnp.bfloat16)[None, None]
     return (
         layer_output,
         input_grad[None, None],

time: 488 us -> 450 us (0.922)
  the two profiles are of different devices: /device:TPU:4 before, /device:TPU:6 now
where the time goes in v2:
time: 450 us; the launch traced here: 441 us
  waiting for transfers between devices  144 us (32%)
  starting transfers between devices  108 us (24%)
  Pallas kernels  83.1 us (18%)
  local copies, waits for them, and re-layouts  48.9 us (11%)
  other arithmetic  33.6 us (7%)
  between operations  16.3 us (4%)
  matrix products  7.64 us (2%)
    ppermute x63, waiting for transfers between devices, send(): lax.ppermute(value, axis, [(i, (i + steps) % count) for i in range(count)])  130 us
    ppermute x63, starting transfers between devices, send(): lax.ppermute(value, axis, [(i, (i + steps) % count) for i in range(count)])  96.7 us
    unnamed x188, local copies, waits for them, and re-layouts  34.4 us
    pallas_call x2, Pallas kernels, outer(): pl.pallas_call(outer_kernel, grid=(wide // size,), in_specs=[pl.BlockSpec...  14.5 us
    pallas_call x1, Pallas kernels, feed(): pl.pallas_call(feed_kernel, grid=(steps,), in_specs=[whole(width), column...  12.9 us
    pallas_call x1, Pallas kernels, attend_back(): pl.pallas_call(functools.partial(attend_back_kernel, heads=heads, group=g...  12.4 us
    ppermute x4, waiting for transfers between devices, shifted(): lax.ppermute(value, axis, [(i, i + steps) for i in range(initial, last)])  11.8 us
    pallas_call x1, Pallas kernels, back(): pl.pallas_call(back_kernel, grid=(columns // size,), in_specs=[pl.BlockSp...  11.3 us
  transfers between devices with their start and end apart: 79, of which 36 were waited for; matrix products, arithmetic and copies ran while one was open for 13% of the time, Pallas kernels for 15%

profile of v2, /device:TPU:6, one launch (start us, length us, event | category | flops | bytes accessed | tf_op | source)
XLA Modules:
  0.0 441.2 jit_solution(13854907903548032)
XLA Ops:
  8.0 4.1 collective-permute-start.3
  19.5 8.9 %collective-permute-done.2 = bf16[64,896]{1,0:T(8,128)(2,1)S(1)} collective-permute-done((bf16[64,896]{1,0:T(8,128)(2,1)S(1)}, bf16[64,896]{1,0:T(8,128)(2,1)S(1)}, u32[]{:S(2)}, u32[]{:S(2)}) %collective-permute-start.2) | collective-permute-done | bytes 114720 | tf_op jit(solution)/shard_map/ppermute | solution.py:24
  28.4 3.4 collective-permute-done
  52.4 4.7 %collective-permute-start.14 = (bf16[64,3072]{1,0:T(8,128)(2,1)}, bf16[64,3072]{1,0:T(8,128)(2,1)}, u32[]{:S(2)}, u32[]{:S(2)}) collective-permute-start(bf16[64,3072]{1,0:T(8,128)(2,1)} %pad_maximum_fusion.17), channel_id=1, source_target_pairs={{0,64},{32,96},{64,0},{96,32},{1,65},{33,97},{65,1},{97,33},{2,66}... | collective-permute-start | bytes 1179656 | tf_op jit(solution)/shard_map/ppermute | solution.py:24
  72.9 9.0 %project.1 = (bf16[512,2048]{1,0:T(8,128)(2,1)S(1)}, bf16[512,512]{1,0:T(8,128)(2,1)S(1)}, bf16[512,256]{1,0:T(8,128)(2,1)S(1)}, f32[512,128]{1,0:T(8,128)S(1)},...) custom-call(s32[8]{0:T(128)S(1)} %pad_add_fusion.info, ...), custom_call_target="tpu_custom_call" | custom-call | tf_op jit(solution)/shard_map/project/pallas_call | solution.py:365
  91.9 4.5 %collective-permute-done.17.refs_1_ = bf16[512,256]{1,0:T(8,128)(2,1)S(1)} collective-permute-done((bf16[512,256]{1,0:T(8,128)(2,1)}, bf16[512,256]{1,0:T(8,128)(2,1)S(1)}, u32[]{:S(2)}, u32[]{:S(2)}) %collective-permute-start.17) | collective-permute-done | bytes 262176 | tf_op jit(solution)/shard_map/ppermute | solution.py:48
  96.4 7.4 %collective-permute-done.16.refs_0_ = bf16[512,256]{1,0:T(8,128)(2,1)S(1)} collective-permute-done((bf16[512,256]{1,0:T(8,128)(2,1)}, bf16[512,256]{1,0:T(8,128)(2,1)S(1)}, u32[]{:S(2)}, u32[]{:S(2)}) %collective-permute-start.16) | collective-permute-done | bytes 262176 | tf_op jit(solution)/shard_map/ppermute | solution.py:48
  103.7 3.7 collective-permute-start.18
  108.4 10.8 %attend.1 = (bf16[512,512]{1,0:T(8,128)(2,1)S(1)}, f32[4,512,128]{2,1,0:T(8,128)S(1)}) custom-call(s32[8]{0:T(128)S(1)} %pad_add_fusion.info, bf16[512,512]{1,0:T(8,128)(2,1)S(1)} %copy-done.23, bf16[512,256]{1,0:T(8,128)(2,1)S(1)} %collective-permute-done.16.refs_0_, bf16[512,256]{1,0:T(8,128)(2,1)S(1)} %collective-permute-done.17.refs_1_, ...), custom_call_target="tpu_custom_call" | custom-call | tf_op jit(solution)/shard_map/attend/pallas_call | solution.py:207
  125.7 5.9 %collective-permute-done.20 = bf16[64,2048]{1,0:T(8,128)(2,1)S(1)} collective-permute-done((bf16[64,2048]{1,0:T(8,128)(2,1)S(1)}, bf16[64,2048]{1,0:T(8,128)(2,1)S(1)}, u32[]{:S(2)}, u32[]{:S(2)}) %collective-permute-start.20) | collective-permute-done | bytes 262176 | tf_op jit(solution)/shard_map/ppermute | solution.py:24
  141.9 5.2 %collective-permute-done.23 = bf16[128,2048]{1,0:T(8,128)(2,1)S(1)} collective-permute-done((bf16[128,2048]{1,0:T(8,128)(2,1)S(1)}, bf16[128,2048]{1,0:T(8,128)(2,1)S(1)}, u32[]{:S(2)}, u32[]{:S(2)}) %collective-permute-start.23) | collective-permute-done | bytes 524320 | tf_op jit(solution)/shard_map/ppermute | solution.py:24
  147.2 3.8 collective-permute-done.21
  154.0 7.5 %collective-permute-done.26 = bf16[128,2048]{1,0:T(8,128)(2,1)S(1)} collective-permute-done((bf16[128,2048]{1,0:T(8,128)(2,1)S(1)}, bf16[128,2048]{1,0:T(8,128)(2,1)S(1)}, u32[]{:S(2)}, u32[]{:S(2)}) %collective-permute-start.26) | collective-permute-done | bytes 524320 | tf_op jit(solution)/shard_map/ppermute | solution.py:24
  161.6 3.8 collective-permute-start.27
  165.4 5.1 %fusion.45.gh_ref = f32[512,1536]{1,0:T(8,128)} fusion(bf16[512,2048]{1,0:T(8,128)(2,1)S(1)} %constant_dynamic-update-slice_fusion.5.right_ref, bf16[1536,2048]{1,0:T(8,128)(2,1)S(1)} %bitcast.192), kind=kOutput, calls=%fused_computation.213 | convolution fusion | flops 3221225472 | bytes 11534336 | tf_op jit(solution)/shard_map/dot_general | solution.py:153
  170.8 7.5 %collective-permute-done.29 = bf16[64,2048]{1,0:T(8,128)(2,1)S(1)} collective-permute-done((bf16[64,2048]{1,0:T(8,128)(2,1)S(1)}, bf16[64,2048]{1,0:T(8,128)(2,1)S(1)}, u32[]{:S(2)}, u32[]{:S(2)}) %collective-permute-start.29) | collective-permute-done | bytes 262176 | tf_op jit(solution)/shard_map/ppermute | solution.py:24
  178.4 12.9 %feed.1 = (bf16[512,1536]{1,0:T(8,128)(2,1)S(1)}, bf16[512,3072]{1,0:T(8,128)(2,1)}) custom-call(bf16[512,2048]{1,0:T(8,128)(2,1)S(1)} %constant_dynamic-update-slice_fusion.10.n_ref.left_ref, f32[512,1536]{1,0:T(8,128)} %fusion.45.gh_ref, bf16[2048,3072]{1,0:T(8,128)(2,1)} %bitcast.195, bf16[2048,3072]{1,0:T(8,128)(2,1)} %bitcast.196), custom_call_target="tpu_custom_call" | custom-call | tf_op jit(solution)/shard_map/feed/pallas_call | solution.py:470
  191.3 4.6 %outer.2 = bf16[1536,2048]{1,0:T(8,128)(2,1)S(1)} custom-call(bf16[512,1536]{1,0:T(8,128)(2,1)S(1)} %get-tuple-element.167.left_ref, bf16[512,2048]{1,0:T(8,128)(2,1)S(1)} %copy-done.14), custom_call_target="tpu_custom_call" | custom-call | tf_op jit(solution)/shard_map/outer/pallas_call | solution.py:519
  201.6 11.3 %back.1 = bf16[512,2048]{1,0:T(8,128)(2,1)S(1)} custom-call(bf16[512,3072]{1,0:T(8,128)(2,1)S(1)} %copy-done.1, bf16[2048,3072]{1,0:T(8,128)(2,1)} %bitcast.197), custom_call_target="tpu_custom_call" | custom-call | tf_op jit(solution)/shard_map/back/pallas_call | solution.py:497
  215.1 4.5 %collective-permute-done.31 = bf16[64,2048]{1,0:T(8,128)(2,1)S(1)} collective-permute-done((bf16[64,2048]{1,0:T(8,128)(2,1)S(1)}, bf16[64,2048]{1,0:T(8,128)(2,1)S(1)}, u32[]{:S(2)}, u32[]{:S(2)}) %collective-permute-start.31) | collective-permute-done | bytes 262176 | tf_op jit(solution)/shard_map/ppermute | solution.py:24
  225.4 10.0 %outer.3 = bf16[2048,3072]{1,0:T(8,128)(2,1)} custom-call(bf16[512,2048]{1,0:T(8,128)(2,1)S(1)} %copy-done.7, bf16[512,3072]{1,0:T(8,128)(2,1)S(1)} %copy-done.1), custom_call_target="tpu_custom_call" | custom-call | tf_op jit(solution)/shard_map/outer/pallas_call | solution.py:519
  249.6 4.5 %times.1 = bf16[512,2048]{1,0:T(8,128)(2,1)S(1)} custom-call(bf16[512,1536]{1,0:T(8,128)(2,1)S(1)} %copy-done.9, bf16[1536,2048]{1,0:T(8,128)(2,1)S(1)} %copy-done.10), custom_call_target="tpu_custom_call" | custom-call | tf_op jit(solution)/shard_map/times/pallas_call | solution.py:543
  264.3 3.8 collective-permute-start.39
  270.9 12.4 %attend_back.1 = (bf16[512,512]{1,0:T(8,128)(2,1)S(1)}, f32[3,512,256]{2,1,0:T(8,128)S(1)}) custom-call(s32[8]{0:T(128)S(1)} %pad_add_fusion.info, bf16[512,512]{1,0:T(8,128)(2,1)S(1)} %copy-done.24, bf16[512,512]{1,0:T(8,128)(2,1)S(1)} %convolution_convert_fusion.do_ref, f32[4,512,128]{2,1,0:T(8,128)S(1)} %copy-done.37, f32[512,128]{1,0:T(8,128)S(1)} %copy-done.21, ...), custom_call_target="tpu_custom_call" | custom-call | tf_op jit(solution)/shard_map/attend_back/pallas_call | solution.py:273
  287.9 3.9 collective-permute-start.44
  293.2 7.7 %collective-permute-done.44 = bf16[48,2048]{1,0:T(8,128)(2,1)S(1)} collective-permute-done((bf16[48,2048]{1,0:T(8,128)(2,1)S(1)}, bf16[48,2048]{1,0:T(8,128)(2,1)S(1)}, u32[]{:S(2)}, u32[]{:S(2)}) %collective-permute-start.44) | collective-permute-done | bytes 196640 | tf_op jit(solution)/shard_map/ppermute | solution.py:24
  308.4 7.7 %unproject.1 = (bf16[512,2048]{1,0:T(8,128)(2,1)S(1)}, bf16[2048,1408]{1,0:T(8,128)(2,1)}) custom-call(bf16[512,512]{1,0:T(8,128)(2,1)S(1)} %get-tuple-element.179.dq_ref, bf16[512,256]{1,0:T(8,128)(2,1)S(1)} %pad_maximum_fusion.22.dkv_ref, bf16[2048,896]{1,0:T(8,128)(2,1)S(1)} %copy-done.12, bf16[512,2048]{1,0:T(8,128)(2,1)S(1)} %copy-done.26, ...), custom_call_target="tpu_custom_call" | custom-call | tf_op jit(solution)/shard_map/unproject/pallas_call | solution.py:420
  325.3 6.9 %collective-permute-done.49 = bf16[48,2048]{1,0:T(8,128)(2,1)} collective-permute-done((bf16[48,2048]{1,0:T(8,128)(2,1)S(1)}, bf16[48,2048]{1,0:T(8,128)(2,1)}, u32[]{:S(2)}, u32[]{:S(2)}) %collective-permute-start.49) | collective-permute-done | bytes 196640 | tf_op jit(solution)/shard_map/ppermute | solution.py:24
  346.1 12.2 %collective-permute-done.54 = bf16[4,16,3072]{2,1,0:T(8,128)(2,1)S(1)} collective-permute-done((bf16[4,16,3072]{2,1,0:T(8,128)(2,1)S(1)}, bf16[4,16,3072]{2,1,0:T(8,128)(2,1)S(1)}, u32[]{:S(2)}, u32[]{:S(2)}) %collective-permute-start.54) | collective-permute-done | bytes 393248 | tf_op jit(solution)/shard_map/ppermute | solution.py:24
  358.3 3.6 collective-permute-done.52
  370.9 9.1 %collective-permute-done.59 = bf16[16,3072]{1,0:T(8,128)(2,1)S(1)} collective-permute-done((bf16[16,3072]{1,0:T(8,128)(2,1)S(1)}, bf16[16,3072]{1,0:T(8,128)(2,1)S(1)}, u32[]{:S(2)}, u32[]{:S(2)}) %collective-permute-start.59) | collective-permute-done | bytes 98336 | tf_op jit(solution)/shard_map/ppermute | solution.py:24
  389.9 6.3 %collective-permute-done.61 = bf16[16,12288]{1,0:T(8,128)(2,1)S(1)} collective-permute-done((bf16[16,12288]{1,0:T(8,128)(2,1)S(1)}, bf16[16,12288]{1,0:T(8,128)(2,1)S(1)}, u32[]{:S(2)}, u32[]{:S(2)}) %collective-permute-start.61) | collective-permute-done | bytes 393248 | tf_op jit(solution)/shard_map/ppermute | solution.py:24
  (446 shorter events, 208.3 us)
Async XLA Ops:
  7.2 39.2 %all-gather.4.cloned.1.call-start = ((), (), s32[]{:S(2)}) async-start(), calls=%async_computation.3 | async-start | bytes 2359296 | tf_op jit(solution)/shard_map/all_gather | solution.py:612
  7.9 113.0 %all-gather.6.cloned.1.call-start = ((), (), s32[]{:S(2)}) async-start(), calls=%async_computation.4 | async-start | bytes 7077888 | tf_op jit(solution)/shard_map/all_gather | solution.py:619
  8.0 23.8 %collective-permute-start.3 = (bf16[128,2048]{1,0:T(8,128)(2,1)}, bf16[128,2048]{1,0:T(8,128)(2,1)S(1)}, u32[]{:S(2)}, u32[]{:S(2)}) collective-permute-start(bf16[128,2048]{1,0:T(8,128)(2,1)} %bitcast.199), channel_id=1, source_target_pairs={{0,96},{32,0},{64,32},{96,64},{1,97},{33,1},{65,33},{97,65},{2,98}... | collective-permute-start | bytes 1572872 | tf_op jit(solution)/shard_map/ppermute | solution.py:24
  12.1 19.7 %collective-permute-start.4 = (bf16[128,2048]{1,0:T(8,128)(2,1)}, bf16[128,2048]{1,0:T(8,128)(2,1)S(1)}, u32[]{:S(2)}, u32[]{:S(2)}) collective-permute-start(bf16[128,2048]{1,0:T(8,128)(2,1)} %bitcast.200), channel_id=1, source_target_pairs={{0,32},{32,64},{64,96},{96,0},{1,33},{33,65},{65,97},{97,1},{2,34}... | collective-permute-start | bytes 1572872 | tf_op jit(solution)/shard_map/ppermute | solution.py:24
  18.0 13.8 %collective-permute-start = (bf16[64,896]{1,0:T(8,128)(2,1)S(1)}, bf16[64,896]{1,0:T(8,128)(2,1)S(1)}, u32[]{:S(2)}, u32[]{:S(2)}) collective-permute-start(bf16[64,896]{1,0:T(8,128)(2,1)S(1)} %get-tuple-element.334), channel_id=1, source_target_pairs={{0,32},{32,64},{64,96},{96,0},{1,33},{33,65},{65,97},{97,1},{2,34}... | collective-permute-start | bytes 344072 | tf_op jit(solution)/shard_map/ppermute | solution.py:24
  31.9 146.6 %all-gather.8.cloned.1.call-start = ((), (), s32[]{:S(2)}) async-start(), calls=%async_computation.5 | async-start | bytes 14155776 | tf_op jit(solution)/shard_map/all_gather | solution.py:641
  51.6 33.1 %collective-permute-start.13 = (bf16[64,3072]{1,0:T(8,128)(2,1)}, bf16[64,3072]{1,0:T(8,128)(2,1)}, u32[]{:S(2)}, u32[]{:S(2)}) collective-permute-start(bf16[64,3072]{1,0:T(8,128)(2,1)} %pad_maximum_fusion.16), channel_id=1, source_target_pairs={{0,32},{32,64},{64,96},{96,0},{1,33},{33,65},{65,97},{97,1},{2,34}... | collective-permute-start | bytes 1179656 | tf_op jit(solution)/shard_map/ppermute | solution.py:24
  52.4 32.3 %collective-permute-start.14 = (bf16[64,3072]{1,0:T(8,128)(2,1)}, bf16[64,3072]{1,0:T(8,128)(2,1)}, u32[]{:S(2)}, u32[]{:S(2)}) collective-permute-start(bf16[64,3072]{1,0:T(8,128)(2,1)} %pad_maximum_fusion.17), channel_id=1, source_target_pairs={{0,64},{32,96},{64,0},{96,32},{1,65},{33,97},{65,1},{97,33},{2,66}... | collective-permute-start | bytes 1179656 | tf_op jit(solution)/shard_map/ppermute | solution.py:24
  64.2 20.5 %collective-permute-start.15 = (bf16[64,3072]{1,0:T(8,128)(2,1)}, bf16[64,3072]{1,0:T(8,128)(2,1)}, u32[]{:S(2)}, u32[]{:S(2)}) collective-permute-start(bf16[64,3072]{1,0:T(8,128)(2,1)} %pad_maximum_fusion.18), channel_id=1, source_target_pairs={{0,96},{32,0},{64,32},{96,64},{1,97},{33,1},{65,33},{97,65},{2,98}... | collective-permute-start | bytes 1179656 | tf_op jit(solution)/shard_map/ppermute | solution.py:24
  88.4 194.9 %reduce-scatter.4.cloned.1.call-start = ((), (), s32[]{:S(2)}) async-start(), calls=%async_computation.6 | async-start | bytes 7077888 | tf_op jit(solution)/shard_map/reduce_scatter | solution.py:610
  103.7 16.4 %collective-permute-start.19 = (bf16[128,2048]{1,0:T(8,128)(2,1)}, bf16[128,2048]{1,0:T(8,128)(2,1)S(1)}, u32[]{:S(2)}, u32[]{:S(2)}) collective-permute-start(bf16[128,2048]{1,0:T(8,128)(2,1)} %bitcast.17), channel_id=1, source_target_pairs={{0,32},{32,64},{64,96},{96,0},{1,33},{33,65},{65,97},{97,1},{2,34}... | collective-permute-start | bytes 1572872 | tf_op jit(solution)/shard_map/ppermute | solution.py:24
  103.7 17.2 %collective-permute-start.18 = (bf16[128,2048]{1,0:T(8,128)(2,1)}, bf16[128,2048]{1,0:T(8,128)(2,1)}, u32[]{:S(2)}, u32[]{:S(2)}) collective-permute-start(bf16[128,2048]{1,0:T(8,128)(2,1)} %bitcast.17), channel_id=1, source_target_pairs={{0,96},{32,0},{64,32},{96,64},{1,97},{33,1},{65,33},{97,65},{2,98}... | collective-permute-start | bytes 1572872 | tf_op jit(solution)/shard_map/ppermute | solution.py:24
  131.8 15.4 %collective-permute-start.23 = (bf16[128,2048]{1,0:T(8,128)(2,1)S(1)}, bf16[128,2048]{1,0:T(8,128)(2,1)S(1)}, u32[]{:S(2)}, u32[]{:S(2)}) collective-permute-start(bf16[128,2048]{1,0:T(8,128)(2,1)S(1)} %pad_maximum_fusion.6), channel_id=1, source_target_pairs={{0,96},{32,0},{64,32},{96,64},{1,97},{33,1},{65,33},{97,65},{2,98}... | collective-permute-start | bytes 1572872 | tf_op jit(solution)/shard_map/ppermute | solution.py:24
  134.8 16.1 %collective-permute-start.21 = (bf16[128,2048]{1,0:T(8,128)(2,1)S(1)}, bf16[128,2048]{1,0:T(8,128)(2,1)S(1)}, u32[]{:S(2)}, u32[]{:S(2)}) collective-permute-start(bf16[128,2048]{1,0:T(8,128)(2,1)S(1)} %pad_maximum_fusion.5), channel_id=1, source_target_pairs={{0,32},{32,64},{64,96},{96,0},{1,33},{33,65},{65,97},{97,1},{2,34}... | collective-permute-start | bytes 1572872 | tf_op jit(solution)/shard_map/ppermute | solution.py:24
  137.5 16.4 %collective-permute-start.25 = (bf16[64,2048]{1,0:T(8,128)(2,1)S(1)}, bf16[64,2048]{1,0:T(8,128)(2,1)S(1)}, u32[]{:S(2)}, u32[]{:S(2)}) collective-permute-start(bf16[64,2048]{1,0:T(8,128)(2,1)S(1)} %slice.276), channel_id=1, source_target_pairs={{0,32},{32,64},{64,96},{96,0},{1,33},{33,65},{65,97},{97,1},{2,34}... | collective-permute-start | bytes 786440 | tf_op jit(solution)/shard_map/ppermute | solution.py:24
  137.6 15.2 %collective-permute-start.24 = (bf16[64,2048]{1,0:T(8,128)(2,1)S(1)}, bf16[64,2048]{1,0:T(8,128)(2,1)S(1)}, u32[]{:S(2)}, u32[]{:S(2)}) collective-permute-start(bf16[64,2048]{1,0:T(8,128)(2,1)S(1)} %slice.275), channel_id=1, source_target_pairs={{0,96},{32,0},{64,32},{96,64},{1,97},{33,1},{65,33},{97,65},{2,98}... | collective-permute-start | bytes 786440 | tf_op jit(solution)/shard_map/ppermute | solution.py:24
  154.0 16.5 %collective-permute-start.28 = (bf16[128,2048]{1,0:T(8,128)(2,1)S(1)}, bf16[128,2048]{1,0:T(8,128)(2,1)S(1)}, u32[]{:S(2)}, u32[]{:S(2)}) collective-permute-start(bf16[128,2048]{1,0:T(8,128)(2,1)S(1)} %get-tuple-element.236), channel_id=1, source_target_pairs={{0,32},{32,64},{64,96},{96,0},{1,33},{33,65},{65,97},{97,1},{2,34}... | collective-permute-start | bytes 1572872 | tf_op jit(solution)/shard_map/ppermute | solution.py:24
  199.8 133.1 %reduce-scatter.6.cloned.1.call-start = ((), (), s32[]{:S(2)}) async-start(), calls=%async_computation.7 | async-start | bytes 14155776 | tf_op jit(solution)/shard_map/reduce_scatter | solution.py:610
  235.4 165.3 %reduce-scatter.8.cloned.1.call-start = ((), (), s32[]{:S(2)}) async-start(), calls=%async_computation.8 | async-start | bytes 6488064 | tf_op jit(solution)/shard_map/reduce_scatter | solution.py:610
  264.3 19.0 %collective-permute-start.39 = (bf16[64,2048]{1,0:T(8,128)(2,1)S(1)}, bf16[64,2048]{1,0:T(8,128)(2,1)}, u32[]{:S(2)}, u32[]{:S(2)}) collective-permute-start(bf16[64,2048]{1,0:T(8,128)(2,1)S(1)} %get-tuple-element.306), channel_id=1, source_target_pairs={{0,96},{32,0},{64,32},{96,64},{1,97},{33,1},{65,33},{97,65},{2,98}... | collective-permute-start | bytes 786440 | tf_op jit(solution)/shard_map/ppermute | solution.py:24
  268.0 15.3 %collective-permute-start.38 = (bf16[64,2048]{1,0:T(8,128)(2,1)S(1)}, bf16[64,2048]{1,0:T(8,128)(2,1)}, u32[]{:S(2)}, u32[]{:S(2)}) collective-permute-start(bf16[64,2048]{1,0:T(8,128)(2,1)S(1)} %get-tuple-element.307), channel_id=1, source_target_pairs={{0,32},{32,64},{64,96},{96,0},{1,33},{33,65},{65,97},{97,1},{2,34}... | collective-permute-start | bytes 786440 | tf_op jit(solution)/shard_map/ppermute | solution.py:24
  283.5 20.7 %collective-permute-start.41 = (bf16[512,256]{1,0:T(8,128)(2,1)S(1)}, bf16[512,256]{1,0:T(8,128)(2,1)S(1)}, u32[]{:S(2)}, u32[]{:S(2)}) collective-permute-start(bf16[512,256]{1,0:T(8,128)(2,1)S(1)} %get-tuple-element.287), channel_id=1, source_target_pairs={{8,0},{12,4},{16,8},{20,12},{24,16},{28,20},{9,1},{13,5},{17,9},{2... | collective-permute-start | bytes 786440 | tf_op jit(solution)/shard_map/ppermute | solution.py:48
  285.1 19.1 %collective-permute-start.40 = (bf16[512,256]{1,0:T(8,128)(2,1)S(1)}, bf16[512,256]{1,0:T(8,128)(2,1)S(1)}, u32[]{:S(2)}, u32[]{:S(2)}) collective-permute-start(bf16[512,256]{1,0:T(8,128)(2,1)S(1)} %get-tuple-element.288), channel_id=1, source_target_pairs={{4,0},{8,4},{12,8},{16,12},{20,16},{24,20},{28,24},{5,1},{9,5},{13... | collective-permute-start | bytes 786440 | tf_op jit(solution)/shard_map/ppermute | solution.py:48
  317.2 15.7 %collective-permute-start.46 = (bf16[64,2048]{1,0:T(8,128)(2,1)}, bf16[64,2048]{1,0:T(8,128)(2,1)}, u32[]{:S(2)}, u32[]{:S(2)}) collective-permute-start(bf16[64,2048]{1,0:T(8,128)(2,1)} %get-tuple-element.247), channel_id=1, source_target_pairs={{0,96},{32,0},{64,32},{96,64},{1,97},{33,1},{65,33},{97,65},{2,98}... | collective-permute-start | bytes 786440 | tf_op jit(solution)/shard_map/ppermute | solution.py:24
  335.2 26.7 %collective-permute-start.50 = (bf16[128,2048]{1,0:T(8,128)(2,1)S(1)}, bf16[128,2048]{1,0:T(8,128)(2,1)S(1)}, u32[]{:S(2)}, u32[]{:S(2)}) collective-permute-start(bf16[128,2048]{1,0:T(8,128)(2,1)S(1)} %pad_maximum_fusion.9), channel_id=1, source_target_pairs={{0,32},{32,64},{64,96},{96,0},{1,33},{33,65},{65,97},{97,1},{2,34}... | collective-permute-start | bytes 1572872 | tf_op jit(solution)/shard_map/ppermute | solution.py:24
  336.4 25.6 %collective-permute-start.51 = (bf16[128,2048]{1,0:T(8,128)(2,1)S(1)}, bf16[128,2048]{1,0:T(8,128)(2,1)S(1)}, u32[]{:S(2)}, u32[]{:S(2)}) collective-permute-start(bf16[128,2048]{1,0:T(8,128)(2,1)S(1)} %pad_maximum_fusion.10), channel_id=1, source_target_pairs={{0,96},{32,0},{64,32},{96,64},{1,97},{33,1},{65,33},{97,65},{2,98}... | collective-permute-start | bytes 1572872 | tf_op jit(solution)/shard_map/ppermute | solution.py:24
  339.8 18.5 %collective-permute-start.54 = (bf16[4,16,3072]{2,1,0:T(8,128)(2,1)S(1)}, bf16[4,16,3072]{2,1,0:T(8,128)(2,1)S(1)}, u32[]{:S(2)}, u32[]{:S(2)}) collective-permute-start(bf16[4,16,3072]{2,1,0:T(8,128)(2,1)S(1)} %get-tuple-element.269), channel_id=1, source_target_pairs={{0,3},{1,0},{2,1},{3,2},{4,7},{5,4},{6,5},{7,6},{8,11},{9,8},{10,9... | collective-permute-start | bytes 1179656 | tf_op jit(solution)/shard_map/ppermute | solution.py:24
  342.2 16.1 %collective-permute-start.53 = (bf16[4,16,3072]{2,1,0:T(8,128)(2,1)S(1)}, bf16[4,16,3072]{2,1,0:T(8,128)(2,1)S(1)}, u32[]{:S(2)}, u32[]{:S(2)}) collective-permute-start(bf16[4,16,3072]{2,1,0:T(8,128)(2,1)S(1)} %get-tuple-element.270), channel_id=1, source_target_pairs={{0,2},{1,3},{2,0},{3,1},{4,6},{5,7},{6,4},{7,5},{8,10},{9,11},{10,... | collective-permute-start | bytes 1179656 | tf_op jit(solution)/shard_map/ppermute | solution.py:24
  342.2 19.7 %collective-permute-start.52 = (bf16[4,16,3072]{2,1,0:T(8,128)(2,1)S(1)}, bf16[4,16,3072]{2,1,0:T(8,128)(2,1)S(1)}, u32[]{:S(2)}, u32[]{:S(2)}) collective-permute-start(bf16[4,16,3072]{2,1,0:T(8,128)(2,1)S(1)} %get-tuple-element.271), channel_id=1, source_target_pairs={{0,1},{1,2},{2,3},{3,0},{4,5},{5,6},{6,7},{7,4},{8,9},{9,10},{10,1... | collective-permute-start | bytes 1179656 | tf_op jit(solution)/shard_map/ppermute | solution.py:24
  363.1 21.8 %collective-permute-start.56 = (bf16[128,2048]{1,0:T(8,128)(2,1)S(1)}, bf16[128,2048]{1,0:T(8,128)(2,1)S(1)}, u32[]{:S(2)}, u32[]{:S(2)}) collective-permute-start(bf16[128,2048]{1,0:T(8,128)(2,1)S(1)} %pad_maximum_fusion.12), channel_id=1, source_target_pairs={{0,96},{32,0},{64,32},{96,64},{1,97},{33,1},{65,33},{97,65},{2,98}... | collective-permute-start | bytes 1572872 | tf_op jit(solution)/shard_map/ppermute | solution.py:24
  365.8 19.0 %collective-permute-start.55 = (bf16[128,2048]{1,0:T(8,128)(2,1)S(1)}, bf16[128,2048]{1,0:T(8,128)(2,1)S(1)}, u32[]{:S(2)}, u32[]{:S(2)}) collective-permute-start(bf16[128,2048]{1,0:T(8,128)(2,1)S(1)} %pad_maximum_fusion.11), channel_id=1, source_target_pairs={{0,32},{32,64},{64,96},{96,0},{1,33},{33,65},{65,97},{97,1},{2,34}... | collective-permute-start | bytes 1572872 | tf_op jit(solution)/shard_map/ppermute | solution.py:24
  369.5 15.4 %collective-permute-start.57 = (bf16[16,3072]{1,0:T(8,128)(2,1)S(1)}, bf16[16,3072]{1,0:T(8,128)(2,1)S(1)}, u32[]{:S(2)}, u32[]{:S(2)}) collective-permute-start(bf16[16,3072]{1,0:T(8,128)(2,1)S(1)} %get-tuple-element.318), channel_id=1, source_target_pairs={{0,32},{32,64},{64,96},{96,0},{1,33},{33,65},{65,97},{97,1},{2,34}... | collective-permute-start | bytes 294920 | tf_op jit(solution)/shard_map/ppermute | solution.py:24
  (132 other events, 1127.2 us)
Sparse Core Ops, SparseCore 0:
  9.8 26.1 all-gather.3
  37.6 43.2 all-gather.5
  88.5 65.9 all-gather.7
  199.9 39.5 reduce-scatter.3
  241.7 79.6 reduce-scatter.5
  323.7 40.8 reduce-scatter.7
